TPU v7x, 32 devices: a whole 2x2x4 slice. The times are simulated.
32 devices in a mesh: row: 4 (over y, x), col: 8 (over z, core).
Axes of the slice: x: 2, y: 2, z: 4, core: 2. Of those that a mesh axis runs over, the one named last changes fastest.
Arguments:
- a_blocks: bfloat16 [8, 4, 16, 32, 128], P('col', 'row'), may hold values from -1 to 1
- a_scale: float32 [8, 4, 16, 4], P('col', 'row'), may hold values from 0.25 to 4
- a_cols: int32 [8, 4, 16, 4], P('col', 'row'), may hold values from 0 to 1023, as said below
- b_blocks: bfloat16 [8, 4, 1024, 32, 128], P('col', 'row'), may hold values from -1 to 1
- b_scale: float32 [8, 4, 1024, 4], P('col', 'row'), may hold values from 0.25 to 4
- b_cols: int32 [8, 4, 1024, 4], P('col', 'row'), may hold values from 0 to 511, as said below
Outputs:
- product: bfloat16 [8, 4, 8, 32, 16384], P('col', 'row')
Inputs may be any that keep to these rules, and one draw needn't show every extreme that they name: `a_cols`: the 4 columns of each block row are distinct. `b_cols`: the 4 columns of each block row are distinct.
All inputs are finite; a program needn't handle non-finite values.
Results may differ from a plain program's by a relative error of at most 0.0034.
Values may be sent and summed in bfloat16 or wider, within the bound.
No kernel may reach another device: no remote copies, remote signals or barrier semaphores. Data moves between devices by JAX's collectives and lax.ppermute only.
A program may use at most 192 MiB of HBM per device.

v0:
```python
import types

import jax
import jax.numpy as jnp
from jax import lax
from jax.experimental import pallas as pl
from jax.experimental.pallas import tpu as pltpu
from jax.sharding import PartitionSpec as P

JW = 512
LANES = 128
META = 16
PARTS = 5
CHUNKS = 4
SLOTS = 8
ROW, COL = "row", "col"
F32, BF16, I32 = jnp.float32, jnp.bfloat16, jnp.int32
VMEM_LIMIT = 12 * 1024 * 1024
SMEM, VMEM, HBM, ANY = pltpu.SMEM, pltpu.VMEM, pltpu.HBM, pl.ANY
DMA = pltpu.SemaphoreType.DMA
copy = pltpu.make_async_copy


def three_parts(x):
    high = x.astype(BF16).astype(F32)
    rest = x - high
    mid = rest.astype(BF16).astype(F32)
    return [high, mid, (rest - mid).astype(BF16).astype(F32)]


def stacked(parts, rows):
    which = lax.broadcasted_iota(I32, (rows, parts[0].shape[1]), 0)
    tile = jnp.zeros(which.shape, F32)
    for at, part in enumerate(parts):
        tile = jnp.where(which == at, jnp.broadcast_to(part, which.shape), tile)
    return tile


def entries(values, first, half, rb):
    ra = values.shape[0]
    one = [values[m : m + 1, first : first + half] for m in range(ra)]
    return jnp.concatenate(one * rb, axis=1)


class Sizes:
    def __init__(self, half, ra, rb, bs):
        self.half, self.ra, self.rb, self.bs = half, ra, rb, bs
        self.wide = ra * bs
        self.tiles = JW * bs // LANES

    def message(self):
        return VMEM((self.half * self.wide + META, self.rb * self.bs), BF16)

    def window(self):
        return VMEM((self.half, self.tiles, self.bs, LANES), F32)


class In:
    def __init__(self, array, place):
        self.array, self.place = array, place
        if place in (VMEM, HBM):
            self.array = pltpu.with_memory_space_constraint(array, place)


def kernel_call(name, body, ins, outs, aliases=(), scratch=None):
    names = list(ins) + list(outs) + list(scratch or {})

    def kernel(*refs):
        body(types.SimpleNamespace(**dict(zip(names, refs))))

    def out_place(shape):
        return ANY if isinstance(shape, jax.ShapeDtypeStruct) else VMEM

    got = pl.pallas_call(
        kernel,
        out_shape=list(outs.values()),
        in_specs=[pl.BlockSpec(memory_space=one.place) for one in ins.values()],
        out_specs=[pl.BlockSpec(memory_space=out_place(shape)) for shape in outs.values()],
        input_output_aliases={list(ins).index(a): list(outs).index(b) for a, b in aliases},
        scratch_shapes=list((scratch or {}).values()),
        compiler_params=pltpu.CompilerParams(vmem_limit_bytes=VMEM_LIMIT),
        cost_estimate=pl.CostEstimate(flops=2 * 10**10, bytes_accessed=1024, transcendentals=0),
        name=name,
    )(*[one.array for one in ins.values()])
    return types.SimpleNamespace(**dict(zip(outs, got)))


class Gather:
    def __init__(self, z, refs, message, flip, which, sem):
        self.z, self.refs, self.message, self.flip, self.which, self.sem = z, refs, message, flip, which, sem

    def start(self):
        z, refs = self.z, self.refs
        cols = refs.cols_s.at[self.which]
        base = (refs.info[0] ^ self.flip) * z.half

        def one_row(i, _):
            for m in range(z.ra):
                at = pl.multiple_of((i * z.ra + m) * z.bs, z.bs)
                copy(refs.b.at[cols[m, base + i]], self.message.at[pl.ds(at, z.bs)], self.sem).start()
            return 0

        lax.fori_loop(0, z.half, one_row, 0, unroll=2)

    def finish(self):
        z, refs = self.z, self.refs
        table, cols = refs.table, refs.cols_v[self.which]
        kw = table.shape[1]
        both = [entries(cols, h * z.half, z.half, z.rb) for h in range(2)]
        named = jnp.where((refs.info[0] ^ self.flip) == 1, both[1], both[0])
        named = jnp.broadcast_to(named, (kw, named.shape[1]))
        picked = lax.broadcasted_iota(I32, named.shape, 0) == named
        picked = jnp.where(picked, 1.0, 0.0).astype(BF16)
        found = jnp.dot(table[...], picked, preferred_element_type=F32)
        slot = lax.broadcasted_iota(I32, (1, found.shape[1]), 1) // (z.ra * z.half)
        parts = []
        for part in range(PARTS):
            value = found[part * z.rb : part * z.rb + 1]
            for n in range(1, z.rb):
                value = jnp.where(slot == n, found[part * z.rb + n : part * z.rb + n + 1], value)
            parts.append(value)
        size = z.half * z.wide
        self.message[pl.ds(size, META), :] = stacked(parts, META).astype(BF16)
        blocks = self.message.at[pl.ds(0, size)]
        copy(blocks, blocks, self.sem).wait()


def add_scratch(z, count=1):
    return dict(
        prods=VMEM((count, z.half * z.wide, LANES), F32),
        scl_v=VMEM((8, LANES), F32),
        col_v=VMEM((8, LANES), I32),
        scl_s=SMEM((8, LANES), F32),
        col_s=SMEM((8, LANES), I32),
        add_sems=DMA((2,)),
    )


class Add:
    def __init__(self, z, refs, pairs):
        self.z, self.refs, self.pairs = z, refs, pairs

    def start(self):
        z, refs = self.z, self.refs
        for at, (a, b) in enumerate(self.pairs):
            a_meta = a[pl.ds(a.shape[0] - META, META), :].astype(F32)
            b_meta = b[pl.ds(b.shape[0] - META, META), :].astype(F32)
            scl_a = a_meta[0:1] + a_meta[1:2] + a_meta[2:3]
            scl_b = b_meta[0:1] + b_meta[1:2] + b_meta[2:3]
            refs.scl_v[at : at + 1, :] = scl_a * scl_b
            refs.col_v[at : at + 1, :] = (b_meta[3:4] * 256.0 + b_meta[4:5]).astype(I32)
        self.moves = [
            copy(refs.scl_v, refs.scl_s, refs.add_sems.at[0]),
            copy(refs.col_v, refs.col_s, refs.add_sems.at[1]),
        ]
        for move in self.moves:
            move.start()
        row_block = lax.broadcasted_iota(I32, (z.wide, z.wide), 0) // z.bs
        col_block = lax.broadcasted_iota(I32, (z.wide, z.wide), 1) // z.bs
        diagonal = jnp.where(row_block == col_block, 1.0, 0.0).astype(BF16)
        for at, (a, b) in enumerate(self.pairs):
            for i in range(z.half):
                left = a[pl.ds(i * z.bs, z.bs), :]
                left = jnp.concatenate([left] * z.ra, axis=0) * diagonal
                rows = pl.ds(i * z.wide, z.wide)
                refs.prods[at, rows, :] = jnp.dot(left, b[rows, :], preferred_element_type=F32)

    def finish(self, after_row=None):
        z, refs, acc = self.z, self.refs, self.refs.acc
        per = LANES // z.bs
        for move in self.moves:
            move.wait()
        lane_block = lax.broadcasted_iota(I32, (8, LANES), 1) // z.bs
        for i in range(z.half):
            for at in range(len(self.pairs)):
                for m in range(z.ra):
                    value = refs.prods[at, pl.ds((i * z.ra + m) * z.bs, z.bs), :]
                    placed = []
                    for n in range(z.rb):
                        entry = (n * z.ra + m) * z.half + i
                        column = refs.col_s[at, entry]
                        place = column & (per - 1)
                        moved = pltpu.roll(value, ((place - n) & (per - 1)) * z.bs, 1)
                        scale = jnp.where(lane_block == place, refs.scl_s[at, entry], 0.0)
                        placed.append((column // per, moved * jnp.concatenate([scale] * (z.bs // 8), axis=0)))
                    for tile, moved in placed:
                        acc[i, tile] = acc[i, tile] + moved
            if after_row is not None:
                after_row(i)


def clear(acc):
    for i in range(acc.shape[0]):

        def clear_tile(tile, _, i=i):
            acc[i, tile] = jnp.zeros(acc.shape[2:], F32)
            return 0

        lax.fori_loop(0, acc.shape[1], clear_tile, 0, unroll=8)


class WriteAll:
    def __init__(self, z, refs):
        self.z, self.refs, self.sent = z, refs, []

    @staticmethod
    def scratch(z):
        return dict(stage=VMEM((SLOTS, z.bs, JW * z.bs // CHUNKS), BF16), out_sems=DMA((SLOTS,)))

    def send(self, at):
        i, chunk = self.sent[at]
        slot, width = at % SLOTS, self.refs.stage.shape[2]
        there = self.refs.out.at[i, :, pl.ds(chunk * width, width)]
        return copy(self.refs.stage.at[slot], there, self.refs.out_sems.at[slot])

    def row(self, i):
        acc, stage = self.refs.acc, self.refs.stage
        tiles = self.z.tiles // CHUNKS
        for chunk in range(CHUNKS):
            at = len(self.sent)
            if at >= SLOTS:
                self.send(at - SLOTS).wait()
            for tile in range(tiles):
                piece = acc[i, chunk * tiles + tile].astype(BF16)
                stage[at % SLOTS, :, pl.ds(tile * LANES, LANES)] = piece
            self.sent.append((i, chunk))
            self.send(at).start()

    def finish(self):
        for at in range(max(0, len(self.sent) - SLOTS), len(self.sent)):
            self.send(at).wait()


def prepare(info, own_cols, b_scl, b_pos):
    rb, kw = b_scl.shape

    def body(refs):
        moves = [
            copy(refs.b_scl, refs.scl, refs.sems.at[0]),
            copy(refs.b_pos, refs.pos, refs.sems.at[1]),
            copy(refs.own_cols, refs.own, refs.sems.at[2]),
        ]
        for move in moves:
            move.start()
        for move in moves:
            move.wait()
        scale, column = refs.scl[...], refs.pos[...]
        table = three_parts(scale) + [(column >> 8).astype(F32), (column & 255).astype(F32)]
        table.append(jnp.zeros((refs.table.shape[0] - PARTS * rb, kw), F32))
        refs.table[...] = jnp.concatenate(table, axis=0).astype(BF16)

    return kernel_call(
        "prepare",
        body,
        dict(info=In(info, SMEM), own_cols=In(own_cols, HBM), b_scl=In(b_scl, HBM), b_pos=In(b_pos, HBM)),
        dict(table=VMEM((-(-PARTS * rb // 16) * 16, kw), BF16), own=VMEM(own_cols.shape, I32)),
        scratch=dict(scl=VMEM(b_scl.shape, F32), pos=VMEM(b_pos.shape, I32), sems=DMA((3,))),
    )


def split(z, info, a, a_scl, after, asked):
    def body(refs):
        scale = refs.a_scl[...]
        both = [entries(scale, h * z.half, z.half, z.rb) for h in range(2)]
        size = z.half * z.bs
        for flip, out in enumerate((refs.kept, refs.given)):
            side = refs.info[0] ^ flip
            out[0, pl.ds(0, size), :] = refs.a[pl.ds(pl.multiple_of(side * size, size), size), :]
            parts = three_parts(jnp.where(side == 1, both[1], both[0]))
            out[0, pl.ds(size, META), :] = stacked(parts, META).astype(BF16)

    piece = VMEM((1, z.half * z.bs + META, z.wide), BF16)
    return kernel_call(
        "split",
        body,
        dict(
            info=In(info, SMEM), a=In(a, VMEM), a_scl=In(a_scl, VMEM), after=In(after, ANY), asked=In(asked, ANY)
        ),
        dict(kept=piece, given=piece),
    )


def join(own, taken):
    count = own.shape[0]

    def body(refs):
        refs.both[pl.ds(0, count)] = refs.own[...]
        refs.both[pl.ds(count, count)] = refs.taken[...]

    outs = dict(both=VMEM((2 * count,) + own.shape[1:], own.dtype))
    return kernel_call("join", body, dict(own=In(own, VMEM), taken=In(taken, VMEM)), outs).both


def answer(z, info, cols, which, flips, table, b, after):
    outs = {"m" + str(flip): z.message() for flip in flips}

    def body(refs):
        gathers = [
            Gather(z, refs, getattr(refs, name), flip, which, refs.sems.at[flip]) for name, flip in zip(outs, flips)
        ]
        for gather in gathers:
            gather.start()
        for gather in gathers:
            gather.finish()

    return kernel_call(
        "answer",
        body,
        dict(
            info=In(info, SMEM),
            cols_s=In(cols, SMEM),
            cols_v=In(cols, VMEM),
            table=In(table, VMEM),
            b=In(b, HBM),
            after=In(after, ANY),
        ),
        outs,
        scratch=dict(sems=DMA((2,))),
    )


def own_blocks(z, info, cols, table, b, kept, after):
    def body(refs):
        answer = Gather(z, refs, refs.message, 1, 0, refs.sems.at[0])
        local = Gather(z, refs, refs.local, 0, 0, refs.sems.at[1])
        local.start()
        answer.start()
        clear(refs.acc)
        local.finish()
        add = Add(z, refs, [(refs.kept.at[0], refs.local)])
        add.start()
        answer.finish()
        add.finish()

    return kernel_call(
        "own_blocks",
        body,
        dict(
            info=In(info, SMEM),
            cols_s=In(cols, SMEM),
            cols_v=In(cols, VMEM),
            table=In(table, VMEM),
            b=In(b, HBM),
            kept=In(kept, VMEM),
            after=In(after, ANY),
        ),
        dict(acc=z.window(), message=z.message()),
        scratch=dict(sems=DMA((2,)), local=z.message(), **add_scratch(z)),
    )


def add_messages(z, info, left, arrived, acc, answer=None, after=None, write=False):
    ins = dict(info=In(info, SMEM), left=In(left, VMEM), acc_in=In(acc, VMEM))
    taken = {"m" + str(at): In(message, VMEM) for at, (_, _, message) in enumerate(arrived)}
    ins.update(taken)
    outs = dict(acc=z.window())
    aliases = [("acc_in", "acc")]
    scratch = add_scratch(z, len(arrived))
    if answer is not None:
        cols, which, side, table, b = answer
        ins.update(cols_s=In(cols, SMEM), cols_v=In(cols, VMEM), table=In(table, VMEM), b=In(b, HBM))
        outs.update(message=z.message())
        scratch.update(sems=DMA((1,)))
    if after is not None:
        ins.update(after=In(after, ANY))
    if write:
        outs.update(out=jax.ShapeDtypeStruct((z.half, z.bs, JW * z.bs), BF16))
        scratch.update(WriteAll.scratch(z))

    def body(refs):
        if answer is not None:
            gather = Gather(z, refs, refs.message, side, which, refs.sems.at[0])
            gather.start()
        pairs = []
        for name, (by, flip, _) in zip(taken, arrived):
            place = flip if by == 0 else refs.info[1 + by] * 2 + flip
            pairs.append((refs.left.at[place], getattr(refs, name)))
        add = Add(z, refs, pairs)
        add.start()
        if answer is not None:
            gather.finish()
        if write:
            writer = WriteAll(z, refs)
            add.finish(writer.row)
            writer.finish()
        else:
            add.finish()

    return kernel_call("add_messages", body, ins, outs, aliases, scratch)


def on_device(a_blocks, a_scale, a_cols, b_blocks, b_scale, b_cols):
    panels = lax.axis_size(ROW)
    columns = lax.axis_size(COL)
    halves = columns // panels
    a_part, a_scl, a_pos = a_blocks[0, 0], a_scale[0, 0].T, a_cols[0, 0].T
    b_part = b_blocks[0, 0]
    b_scl, b_pos = b_scale[0, 0].T, b_cols[0, 0].T
    nrows, bs, _ = a_part.shape
    z = Sizes(nrows // halves, a_scl.shape[0], b_scl.shape[0], bs)
    row = lax.axis_index(ROW)
    parity = lax.axis_index(COL) % halves
    info = jnp.stack([parity] + [row ^ ((row - by) % panels) for by in range(panels)]).astype(I32)

    def step(value, by, flip):
        pairs = [
            (c, ((c // halves + by) % panels) * halves + (c % halves ^ flip)) for c in range(columns)
        ]
        return lax.ppermute(value, COL, pairs)

    def named_by(by, cols):
        pairs = []
        for r in range(panels):
            for c in range(columns):
                to_row = (r + by) % panels
                to_col = (c - halves * by) % columns
                pairs.append((r * columns + c, to_row * columns + to_col))
        return lax.ppermute(cols, (ROW, COL), pairs)

    order = sorted(range(1, panels), key=lambda by: -min(by, panels - by))
    last = order[-1]
    own_cols = a_pos[None]

    first_cols = named_by(order[0], own_cols)
    ready = prepare(info, own_cols, b_scl, b_pos)
    own_cols, table = ready.own, ready.table
    cols = join(own_cols, first_cols)
    asked, known, by = {0: (own_cols, 0)}, [0, order[0]], panels // 4
    more_cols = named_by(by, cols)
    got = answer(z, info, cols, 1, (0, 1), table, b_part, table)
    after = got.m0
    moving = {(order[0], flip): step(one, order[0], flip) for flip, one in enumerate((got.m0, got.m1))}
    pieces = split(z, info, a_part.reshape(nrows * bs, z.wide), a_scl, after, more_cols)
    while True:
        asked.update({(to + by) % panels: (more_cols, at) for at, to in enumerate(known)})
        known += [(to + by) % panels for to in known]
        by //= 2
        if not by:
            break
        cols = join(cols, more_cols)
        more_cols = named_by(by, cols)

    own_left = join(pieces.kept, step(pieces.given, 0, 1))
    left = own_left
    bit = 1
    while bit < panels:
        left = join(left, lax.ppermute(left, ROW, [(r, r ^ bit) for r in range(panels)]))
        bit *= 2

    mine = own_blocks(z, info, own_cols, table, b_part, pieces.kept, after)
    taken = step(mine.message, 0, 1)
    after = mine.message
    for by in order[1:-1]:
        for flip in range(halves):
            got = answer(z, info, *asked[by], (flip,), table, b_part, after)
            (after,) = vars(got).values()
            moving[by, flip] = step(after, by, flip)

    got = add_messages(
        z, info, own_left, [(0, 1, taken)], mine.acc, (*asked[last], 0, table, b_part), after=after
    )
    acc, ends = got.acc, [got.message]
    early = [(by, flip) for by in order[:-1] for flip in range(halves)]
    for at, (by, flip) in enumerate(early[:-1]):
        got = add_messages(
            z, info, left, [(by, flip, moving[by, flip])], acc,
            (*asked[last], 1, table, b_part) if at == 0 else None, after=ends[0] if at == 0 else None,
        )
        acc = got.acc
        if at == 0:
            ends.append(got.message)
    final = [(*early[-1], moving[early[-1]])]
    final += [(last, flip, step(ends[flip], last, flip)) for flip in range(halves)]
    out = add_messages(z, info, left, final, acc, write=True).out
    return out[None, None]


def solution(mesh):
    in_specs = (
        P(COL, ROW, None, None, None),
        P(COL, ROW, None, None),
        P(COL, ROW, None, None),
        P(COL, ROW, None, None, None),
        P(COL, ROW, None, None),
        P(COL, ROW, None, None),
    )
    out_specs = P(COL, ROW, None, None, None)
    return jax.shard_map(
        on_device, mesh=mesh, in_specs=in_specs, out_specs=out_specs, check_vma=False
    )
```

profile of v0, /device:TPU:0, one launch (start us, length us, event | category | flops | bytes accessed | tf_op | source)
XLA Modules:
  0.0 69.0 jit_solution(16011538804287814341)
XLA Ops:
  0.0 5.0 %collective-permute-start = (s32[1,4,16]{2,1,0:T(4,128)}, s32[1,4,16]{2,1,0:T(4,128)S(1)}, u32[]{:S(2)}, u32[]{:S(2)}) collective-permute-start(s32[1,4,16]{2,1,0:T(4,128)} %bitcast.32), channel_id=1, source_target_pairs={{0,20},{1,21},{2,22},{3,23},{4,16},{5,17},{6,18},{7,19},{8,28},{9,... | collective-permute-start | bytes 776 | tf_op jit(solution)/shard_map/ppermute | solution.py:418
  5.0 0.1 stack.23.refs_0_
  5.1 1.3 %prepare.1 = (bf16[32,1024]{1,0:T(8,128)(2,1)S(1)}, s32[1,4,16]{2,1,0:T(4,128)S(1)}) custom-call(s32[5]{0:T(128)S(1)} %stack.23.refs_0_, s32[1,4,16]{2,1,0:T(4,128)} %bitcast.33, f32[4,1024]{1,0:T(4,128)} %bitcast.30, s32[4,1024]{1,0:T(4,128)} %bitcast.31), custom_call_target="tpu_custom_call" | custom-call | flops 20000000000 | bytes 1024 | tf_op jit(solution)/shard_map/prepare/pallas_call | solution.py:74
  6.4 0.4 collective-permute-done.refs_1_
  6.8 4.8 %collective-permute-start.1 = (s32[2,4,16]{2,1,0:T(4,128)S(1)}, s32[2,4,16]{2,1,0:T(4,128)S(1)}, u32[]{:S(2)}, u32[]{:S(2)}) collective-permute-start(s32[2,4,16]{2,1,0:T(4,128)S(1)} %join.4.refs_1_.refs_2_), channel_id=1, source_target_pairs={{0,14},{1,15},{2,8},{3,9},{4,10},{5,11},{6,12},{7,13},{8,22},{9,23... | collective-permute-start | bytes 1544 | tf_op jit(solution)/shard_map/ppermute | solution.py:418
  11.6 0.0 copy-start
  11.6 0.0 copy-start.1
  11.6 2.6 %answer.3 = (bf16[1040,128]{1,0:T(8,128)(2,1)}, bf16[1040,128]{1,0:T(8,128)(2,1)}) custom-call(s32[5]{0:T(128)S(1)} %stack.23.refs_0_, s32[2,4,16]{2,1,0:T(4,128)S(1)} %join.4.refs_1_.refs_2_, s32[2,4,16]{2,1,0:T(4,128)S(1)} %join.4.refs_1_.refs_2_, bf16[32,1024]{1,0:T(8,128)(2,1)S(1)} %get-tuple-element.19.refs_3_.refs_5_.refs_6_, ...), custom_call_target="tpu_custom_call" | custom-call | flops 20000000000 | bytes 1024 | tf_op jit(solution)/shard_map/answer/pallas_call | solution.py:74
  14.2 0.1 collective-permute-start.7
  14.3 0.9 %collective-permute-start.6 = (bf16[1040,128]{1,0:T(8,128)(2,1)}, bf16[1040,128]{1,0:T(8,128)(2,1)}, u32[]{:S(2)}, u32[]{:S(2)}) collective-permute-start(bf16[1040,128]{1,0:T(8,128)(2,1)} %get-tuple-element.20.refs_3_.refs_6_), channel_id=1, source_target_pairs={{0,4},{1,5},{2,6},{3,7},{4,0},{5,1},{6,2},{7,3},{8,12},{9,13},{10,... | collective-permute-start | bytes 798728 | tf_op jit(solution)/shard_map/ppermute | solution.py:409
  15.2 0.0 collective-permute-done.1.refs_4_.refs_1_.refs_2_.refs_5_
  15.2 0.0 copy-done
  15.2 0.0 copy-done.1
  15.2 0.6 split.1
  15.9 1.9 %collective-permute-start.2 = (bf16[1,272,128]{2,1,0:T(8,128)(2,1)S(1)}, bf16[1,272,128]{2,1,0:T(8,128)(2,1)S(1)}, u32[]{:S(2)}, u32[]{:S(2)}) collective-permute-start(bf16[1,272,128]{2,1,0:T(8,128)(2,1)S(1)} %get-tuple-element.22), channel_id=1, source_target_pairs={{0,1},{1,0},{2,3},{3,2},{4,5},{5,4},{6,7},{7,6},{8,9},{9,8},{10,11... | collective-permute-start | bytes 208904 | tf_op jit(solution)/shard_map/ppermute | solution.py:409
  17.8 4.2 %own_blocks.1 = (f32[8,128,32,128]{3,2,1,0:T(8,128)S(1)}, bf16[1040,128]{1,0:T(8,128)(2,1)S(1)}) custom-call(s32[5]{0:T(128)S(1)} %stack.23.refs_0_, s32[1,4,16]{2,1,0:T(4,128)S(1)} %get-tuple-element.18.refs_0_.refs_1_.refs_2_, s32[1,4,16]{2,1,0:T(4,128)S(1)} %get-tuple-element.18.refs_0_.refs_1_.refs_2_, ...), custom_call_target="tpu_custom_call" | custom-call | flops 20000000000 | bytes 1024 | tf_op jit(solution)/shard_map/own_blocks/pallas_call | solution.py:74
  22.0 0.1 collective-permute-start.5
  22.1 1.6 %answer.4.refs_5_ = bf16[1040,128]{1,0:T(8,128)(2,1)S(1)} custom-call(s32[5]{0:T(128)S(1)} %stack.23.refs_0_, s32[2,4,16]{2,1,0:T(4,128)S(1)} %collective-permute-done.1.refs_4_.refs_1_.refs_2_.refs_5_, s32[2,4,16]{2,1,0:T(4,128)S(1)} %collective-permute-done.1.refs_4_.refs_1_.refs_2_.refs_5_, ...), custom_call_target="tpu_custom_call" | custom-call | flops 20000000000 | bytes 1024 | tf_op jit(solution)/shard_map/answer/pallas_call | solution.py:74
  23.7 0.1 collective-permute-start.8
  23.7 0.0 collective-permute-done.2.refs_1_
  23.8 1.6 %collective-permute-start.3 = (bf16[2,272,128]{2,1,0:T(8,128)(2,1)S(1)}, bf16[2,272,128]{2,1,0:T(8,128)(2,1)S(1)}, u32[]{:S(2)}, u32[]{:S(2)}) collective-permute-start(bf16[2,272,128]{2,1,0:T(8,128)(2,1)S(1)} %join.5.refs_0_.refs_1_), channel_id=1, source_target_pairs={{0,8},{8,0},{16,24},{24,16},{1,9},{9,1},{17,25},{25,17},{2,10},{10... | collective-permute-start | bytes 417800 | tf_op jit(solution)/shard_map/ppermute | solution.py:447
  25.3 1.6 %answer.5.refs_8_ = bf16[1040,128]{1,0:T(8,128)(2,1)S(1)} custom-call(s32[5]{0:T(128)S(1)} %stack.23.refs_0_, s32[2,4,16]{2,1,0:T(4,128)S(1)} %collective-permute-done.1.refs_4_.refs_1_.refs_2_.refs_5_, s32[2,4,16]{2,1,0:T(4,128)S(1)} %collective-permute-done.1.refs_4_.refs_1_.refs_2_.refs_5_, ...), custom_call_target="tpu_custom_call" | custom-call | flops 20000000000 | bytes 1024 | tf_op jit(solution)/shard_map/answer/pallas_call | solution.py:74
  26.9 3.0 %collective-permute-done.3.refs_1_ = bf16[2,272,128]{2,1,0:T(8,128)(2,1)S(1)} collective-permute-done((bf16[2,272,128]{2,1,0:T(8,128)(2,1)S(1)}, bf16[2,272,128]{2,1,0:T(8,128)(2,1)S(1)}, u32[]{:S(2)}, u32[]{:S(2)}) %collective-permute-start.3) | collective-permute-done | bytes 139296 | tf_op jit(solution)/shard_map/ppermute | solution.py:447
  29.9 0.0 collective-permute-start.9
  29.9 0.0 collective-permute-done.5.refs_3_
  30.0 1.6 %collective-permute-start.4 = (bf16[4,272,128]{2,1,0:T(8,128)(2,1)S(1)}, bf16[4,272,128]{2,1,0:T(8,128)(2,1)S(1)}, u32[]{:S(2)}, u32[]{:S(2)}) collective-permute-start(bf16[4,272,128]{2,1,0:T(8,128)(2,1)S(1)} %join.6.refs_0_), channel_id=1, source_target_pairs={{0,16},{8,24},{16,0},{24,8},{1,17},{9,25},{17,1},{25,9},{2,18},{10... | collective-permute-start | bytes 835592 | tf_op jit(solution)/shard_map/ppermute | solution.py:447
  31.5 2.6 %add_messages.5 = (f32[8,128,32,128]{3,2,1,0:T(8,128)S(1)}, bf16[1040,128]{1,0:T(8,128)(2,1)S(1)}) custom-call(s32[5]{0:T(128)S(1)} %stack.23.refs_0_, bf16[2,272,128]{2,1,0:T(8,128)(2,1)S(1)} %join.5.refs_0_.refs_1_, f32[8,128,32,128]{3,2,1,0:T(8,128)S(1)} %get-tuple-element.23.refs_2_, ...), custom_call_target="tpu_custom_call", output_to_operand_aliasing={{0}: (2, {})} | custom-call | flops 20000000000 | bytes 1024 | tf_op jit(solution)/shard_map/add_messages/pallas_call | solution.py:74
  34.1 5.1 %collective-permute-done.4.refs_1_ = bf16[4,272,128]{2,1,0:T(8,128)(2,1)S(1)} collective-permute-done((bf16[4,272,128]{2,1,0:T(8,128)(2,1)S(1)}, bf16[4,272,128]{2,1,0:T(8,128)(2,1)S(1)}, u32[]{:S(2)}, u32[]{:S(2)}) %collective-permute-start.4) | collective-permute-done | bytes 278560 | tf_op jit(solution)/shard_map/ppermute | solution.py:447
  39.2 3.3 %collective-permute-start.10 = (bf16[1040,128]{1,0:T(8,128)(2,1)S(1)}, bf16[1040,128]{1,0:T(8,128)(2,1)S(1)}, u32[]{:S(2)}, u32[]{:S(2)}) collective-permute-start(bf16[1040,128]{1,0:T(8,128)(2,1)S(1)} %get-tuple-element.26.refs_8_), channel_id=1, source_target_pairs={{0,6},{1,7},{2,0},{3,1},{4,2},{5,3},{6,4},{7,5},{8,14},{9,15},{10,... | collective-permute-start | bytes 798728 | tf_op jit(solution)/shard_map/ppermute | solution.py:409
  42.6 8.0 %collective-permute-done.6.refs_3_ = bf16[1040,128]{1,0:T(8,128)(2,1)} collective-permute-done((bf16[1040,128]{1,0:T(8,128)(2,1)}, bf16[1040,128]{1,0:T(8,128)(2,1)}, u32[]{:S(2)}, u32[]{:S(2)}) %collective-permute-start.6) | collective-permute-done | bytes 266272 | tf_op jit(solution)/shard_map/ppermute | solution.py:409
  50.6 2.9 %add_messages.6 = (f32[8,128,32,128]{3,2,1,0:T(8,128)S(1)}, bf16[1040,128]{1,0:T(8,128)(2,1)S(1)}) custom-call(s32[5]{0:T(128)S(1)} %stack.23.refs_0_, bf16[8,272,128]{2,1,0:T(8,128)(2,1)S(1)} %join.7.refs_1_, f32[8,128,32,128]{3,2,1,0:T(8,128)S(1)} %get-tuple-element.25.refs_2_, ...), custom_call_target="tpu_custom_call", output_to_operand_aliasing={{0}: (2, {})} | custom-call | flops 20000000000 | bytes 1024 | tf_op jit(solution)/shard_map/add_messages/pallas_call | solution.py:74
  53.5 0.2 collective-permute-start.11
  53.8 0.0 collective-permute-done.7.refs_3_
  53.8 2.6 %add_messages.7.refs_2_ = f32[8,128,32,128]{3,2,1,0:T(8,128)S(1)} custom-call(s32[5]{0:T(128)S(1)} %stack.23.refs_0_, bf16[8,272,128]{2,1,0:T(8,128)(2,1)S(1)} %join.7.refs_1_, f32[8,128,32,128]{3,2,1,0:T(8,128)S(1)} %get-tuple-element.27.refs_2_, bf16[1040,128]{1,0:T(8,128)(2,1)} %collective-permute-done.7.refs_3_), custom_call_target="tpu_custom_call", output_to_operand_aliasing={{}: (2, {})} | custom-call | flops 20000000000 | bytes 1024 | tf_op jit(solution)/shard_map/add_messages/pallas_call | solution.py:74
  56.4 0.0 collective-permute-done.8.refs_3_
  56.4 2.2 %add_messages.8.refs_2_ = f32[8,128,32,128]{3,2,1,0:T(8,128)S(1)} custom-call(s32[5]{0:T(128)S(1)} %stack.23.refs_0_, bf16[8,272,128]{2,1,0:T(8,128)(2,1)S(1)} %join.7.refs_1_, f32[8,128,32,128]{3,2,1,0:T(8,128)S(1)} %add_messages.7.refs_2_, bf16[1040,128]{1,0:T(8,128)(2,1)S(1)} %collective-permute-done.8.refs_3_), custom_call_target="tpu_custom_call", output_to_operand_aliasing={{}: (2, {})} | custom-call | flops 20000000000 | bytes 1024 | tf_op jit(solution)/shard_map/add_messages/pallas_call | solution.py:74
  58.7 0.0 collective-permute-done.9.refs_3_
  58.7 0.0 collective-permute-done.10.refs_4_
  58.7 3.5 %collective-permute-done.11.refs_5_ = bf16[1040,128]{1,0:T(8,128)(2,1)S(1)} collective-permute-done((bf16[1040,128]{1,0:T(8,128)(2,1)S(1)}, bf16[1040,128]{1,0:T(8,128)(2,1)S(1)}, u32[]{:S(2)}, u32[]{:S(2)}) %collective-permute-start.11) | collective-permute-done | bytes 266272 | tf_op jit(solution)/shard_map/ppermute | solution.py:409
  62.2 6.6 %add_messages.9 = (f32[8,128,32,128]{3,2,1,0:T(8,128)S(1)}, bf16[8,32,16384]{2,1,0:T(8,128)(2,1)}) custom-call(s32[5]{0:T(128)S(1)} %stack.23.refs_0_, bf16[8,272,128]{2,1,0:T(8,128)(2,1)S(1)} %join.7.refs_1_, f32[8,128,32,128]{3,2,1,0:T(8,128)S(1)} %add_messages.8.refs_2_, ...), custom_call_target="tpu_custom_call", output_to_operand_aliasing={{0}: (2, {})} | custom-call | flops 20000000000 | bytes 1024 | tf_op jit(solution)/shard_map/add_messages/pallas_call | solution.py:74
  (4 shorter events, 0.1 us)
Async XLA Ops:
  0.0 6.8 %collective-permute-start = (s32[1,4,16]{2,1,0:T(4,128)}, s32[1,4,16]{2,1,0:T(4,128)S(1)}, u32[]{:S(2)}, u32[]{:S(2)}) collective-permute-start(s32[1,4,16]{2,1,0:T(4,128)} %bitcast.32), channel_id=1, source_target_pairs={{0,20},{1,21},{2,22},{3,23},{4,16},{5,17},{6,18},{7,19},{8,28},{9,... | collective-permute-start | bytes 776 | tf_op jit(solution)/shard_map/ppermute | solution.py:418
  6.8 8.5 %collective-permute-start.1 = (s32[2,4,16]{2,1,0:T(4,128)S(1)}, s32[2,4,16]{2,1,0:T(4,128)S(1)}, u32[]{:S(2)}, u32[]{:S(2)}) collective-permute-start(s32[2,4,16]{2,1,0:T(4,128)S(1)} %join.4.refs_1_.refs_2_), channel_id=1, source_target_pairs={{0,14},{1,15},{2,8},{3,9},{4,10},{5,11},{6,12},{7,13},{8,22},{9,23... | collective-permute-start | bytes 1544 | tf_op jit(solution)/shard_map/ppermute | solution.py:418
  11.6 3.7 %copy-start = (bf16[1,1,16,32,128]{4,3,2,1,0:T(8,128)(2,1)S(1)}, bf16[1,1,16,32,128]{4,3,2,1,0:T(8,128)(2,1)}, u32[]{:S(2)}) copy-start(bf16[1,1,16,32,128]{4,3,2,1,0:T(8,128)(2,1)} %param.6) | copy-start | bytes 393220
  11.6 3.7 %copy-start.1 = (f32[1,1,16,4]{2,3,1,0:T(4,128)S(1)}, f32[1,1,16,4]{2,3,1,0:T(4,128)}, u32[]{:S(2)}) copy-start(f32[1,1,16,4]{2,3,1,0:T(4,128)} %param.7) | copy-start | bytes 772
  14.2 39.5 %collective-permute-start.7 = (bf16[1040,128]{1,0:T(8,128)(2,1)}, bf16[1040,128]{1,0:T(8,128)(2,1)}, u32[]{:S(2)}, u32[]{:S(2)}) collective-permute-start(bf16[1040,128]{1,0:T(8,128)(2,1)} %get-tuple-element.28), channel_id=1, source_target_pairs={{0,5},{1,4},{2,7},{3,6},{4,1},{5,0},{6,3},{7,2},{8,13},{9,12},{10,... | collective-permute-start | bytes 798728 | tf_op jit(solution)/shard_map/ppermute | solution.py:409
  14.3 36.3 %collective-permute-start.6 = (bf16[1040,128]{1,0:T(8,128)(2,1)}, bf16[1040,128]{1,0:T(8,128)(2,1)}, u32[]{:S(2)}, u32[]{:S(2)}) collective-permute-start(bf16[1040,128]{1,0:T(8,128)(2,1)} %get-tuple-element.20.refs_3_.refs_6_), channel_id=1, source_target_pairs={{0,4},{1,5},{2,6},{3,7},{4,0},{5,1},{6,2},{7,3},{8,12},{9,13},{10,... | collective-permute-start | bytes 798728 | tf_op jit(solution)/shard_map/ppermute | solution.py:409
  15.9 7.9 %collective-permute-start.2 = (bf16[1,272,128]{2,1,0:T(8,128)(2,1)S(1)}, bf16[1,272,128]{2,1,0:T(8,128)(2,1)S(1)}, u32[]{:S(2)}, u32[]{:S(2)}) collective-permute-start(bf16[1,272,128]{2,1,0:T(8,128)(2,1)S(1)} %get-tuple-element.22), channel_id=1, source_target_pairs={{0,1},{1,0},{2,3},{3,2},{4,5},{5,4},{6,7},{7,6},{8,9},{9,8},{10,11... | collective-permute-start | bytes 208904 | tf_op jit(solution)/shard_map/ppermute | solution.py:409
  22.0 7.9 %collective-permute-start.5 = (bf16[1040,128]{1,0:T(8,128)(2,1)S(1)}, bf16[1040,128]{1,0:T(8,128)(2,1)S(1)}, u32[]{:S(2)}, u32[]{:S(2)}) collective-permute-start(bf16[1040,128]{1,0:T(8,128)(2,1)S(1)} %get-tuple-element.24.refs_5_), channel_id=1, source_target_pairs={{0,1},{1,0},{2,3},{3,2},{4,5},{5,4},{6,7},{7,6},{8,9},{9,8},{10,11... | collective-permute-start | bytes 798728 | tf_op jit(solution)/shard_map/ppermute | solution.py:409
  23.7 32.8 %collective-permute-start.8 = (bf16[1040,128]{1,0:T(8,128)(2,1)S(1)}, bf16[1040,128]{1,0:T(8,128)(2,1)S(1)}, u32[]{:S(2)}, u32[]{:S(2)}) collective-permute-start(bf16[1040,128]{1,0:T(8,128)(2,1)S(1)} %answer.4.refs_5_), channel_id=1, source_target_pairs={{0,2},{1,3},{2,4},{3,5},{4,6},{5,7},{6,0},{7,1},{8,10},{9,11},{10,... | collective-permute-start | bytes 798728 | tf_op jit(solution)/shard_map/ppermute | solution.py:409
  23.8 6.1 %collective-permute-start.3 = (bf16[2,272,128]{2,1,0:T(8,128)(2,1)S(1)}, bf16[2,272,128]{2,1,0:T(8,128)(2,1)S(1)}, u32[]{:S(2)}, u32[]{:S(2)}) collective-permute-start(bf16[2,272,128]{2,1,0:T(8,128)(2,1)S(1)} %join.5.refs_0_.refs_1_), channel_id=1, source_target_pairs={{0,8},{8,0},{16,24},{24,16},{1,9},{9,1},{17,25},{25,17},{2,10},{10... | collective-permute-start | bytes 417800 | tf_op jit(solution)/shard_map/ppermute | solution.py:447
  29.9 28.8 %collective-permute-start.9 = (bf16[1040,128]{1,0:T(8,128)(2,1)S(1)}, bf16[1040,128]{1,0:T(8,128)(2,1)S(1)}, u32[]{:S(2)}, u32[]{:S(2)}) collective-permute-start(bf16[1040,128]{1,0:T(8,128)(2,1)S(1)} %answer.5.refs_8_), channel_id=1, source_target_pairs={{0,3},{1,2},{2,5},{3,4},{4,7},{5,6},{6,1},{7,0},{8,11},{9,10},{10,... | collective-permute-start | bytes 798728 | tf_op jit(solution)/shard_map/ppermute | solution.py:409
  30.0 9.3 %collective-permute-start.4 = (bf16[4,272,128]{2,1,0:T(8,128)(2,1)S(1)}, bf16[4,272,128]{2,1,0:T(8,128)(2,1)S(1)}, u32[]{:S(2)}, u32[]{:S(2)}) collective-permute-start(bf16[4,272,128]{2,1,0:T(8,128)(2,1)S(1)} %join.6.refs_0_), channel_id=1, source_target_pairs={{0,16},{8,24},{16,0},{24,8},{1,17},{9,25},{17,1},{25,9},{2,18},{10... | collective-permute-start | bytes 835592 | tf_op jit(solution)/shard_map/ppermute | solution.py:447
  39.2 19.4 %collective-permute-start.10 = (bf16[1040,128]{1,0:T(8,128)(2,1)S(1)}, bf16[1040,128]{1,0:T(8,128)(2,1)S(1)}, u32[]{:S(2)}, u32[]{:S(2)}) collective-permute-start(bf16[1040,128]{1,0:T(8,128)(2,1)S(1)} %get-tuple-element.26.refs_8_), channel_id=1, source_target_pairs={{0,6},{1,7},{2,0},{3,1},{4,2},{5,3},{6,4},{7,5},{8,14},{9,15},{10,... | collective-permute-start | bytes 798728 | tf_op jit(solution)/shard_map/ppermute | solution.py:409
  53.5 8.7 %collective-permute-start.11 = (bf16[1040,128]{1,0:T(8,128)(2,1)S(1)}, bf16[1040,128]{1,0:T(8,128)(2,1)S(1)}, u32[]{:S(2)}, u32[]{:S(2)}) collective-permute-start(bf16[1040,128]{1,0:T(8,128)(2,1)S(1)} %get-tuple-element.29), channel_id=1, source_target_pairs={{0,7},{1,6},{2,1},{3,0},{4,3},{5,2},{6,5},{7,4},{8,15},{9,14},{10,... | collective-permute-start | bytes 798728 | tf_op jit(solution)/shard_map/ppermute | solution.py:409
where the time goes:
time: 69.5 us; the launch traced here: 69 us
  Pallas kernels  29 us (42%)
  waiting for transfers between devices  20.1 us (29%)
  starting transfers between devices  19.5 us (28%)
    pallas_call x15, Pallas kernels, kernel_call(): pl.pallas_call(kernel, out_shape=list(outs.values()), in_specs=[pl.BlockS...  29 us
    ppermute x8, waiting for transfers between devices, step(): return lax.ppermute(value, COL, pairs)  11.6 us
    ppermute x2, starting transfers between devices, named_by(): return lax.ppermute(cols, (ROW, COL), pairs)  9.8 us
    ppermute x2, waiting for transfers between devices, on_device(): lax.ppermute(left, ROW, [(r, r ^ bit) for r in range(panels)])  8.13 us
    ppermute x8, starting transfers between devices, step(): return lax.ppermute(value, COL, pairs)  6.56 us
    ppermute x2, starting transfers between devices, on_device(): lax.ppermute(left, ROW, [(r, r ^ bit) for r in range(panels)])  3.14 us
  transfers between devices with their start and end apart: 12, of which 5 were waited for; matrix products, arithmetic and copies ran while one was open for 0% of the time, Pallas kernels for 32%

commit v1 on v0

--- a/solution.py
+++ b/solution.py
@@ -461,6 +461,7 @@
     )
     acc, ends = got.acc, [got.message]
     early = [(by, flip) for by in order[:-1] for flip in range(halves)]
+    early[:halves] = early[halves - 1 :: -1]
     for at, (by, flip) in enumerate(early[:-1]):
         got = add_messages(
             z, info, left, [(by, flip, moving[by, flip])], acc,

time: 69.5 us -> 69.1 us (level)
  transfers between devices with their start and end apart: 12 -> 12, of which waited for: 5 -> 7; matrix products, arithmetic and copies ran while one was open for 0% -> 0% of each run, Pallas kernels for 32% -> 33%
where the time goes in v1:
time: 69.1 us; the launch traced here: 68.6 us
  Pallas kernels  29 us (42%)
  waiting for transfers between devices  19.7 us (29%)
  starting transfers between devices  19.5 us (28%)
    pallas_call x15, Pallas kernels, kernel_call(): pl.pallas_call(kernel, out_shape=list(outs.values()), in_specs=[pl.BlockS...  29 us
    ppermute x8, waiting for transfers between devices, step(): return lax.ppermute(value, COL, pairs)  11.2 us
    ppermute x2, starting transfers between devices, named_by(): return lax.ppermute(cols, (ROW, COL), pairs)  9.8 us
    ppermute x2, waiting for transfers between devices, on_device(): lax.ppermute(left, ROW, [(r, r ^ bit) for r in range(panels)])  8.13 us
    ppermute x8, starting transfers between devices, step(): return lax.ppermute(value, COL, pairs)  6.56 us
    ppermute x2, starting transfers between devices, on_device(): lax.ppermute(left, ROW, [(r, r ^ bit) for r in range(panels)])  3.14 us
  transfers between devices with their start and end apart: 12, of which 7 were waited for; matrix products, arithmetic and copies ran while one was open for 0% of the time, Pallas kernels for 33%

profile of v1, /device:TPU:0, one launch (start us, length us, event | category | flops | bytes accessed | tf_op | source)
XLA Modules:
  0.0 68.6 jit_solution(11827785046490659528)
XLA Ops:
  0.0 5.0 %collective-permute-start = (s32[1,4,16]{2,1,0:T(4,128)}, s32[1,4,16]{2,1,0:T(4,128)S(1)}, u32[]{:S(2)}, u32[]{:S(2)}) collective-permute-start(s32[1,4,16]{2,1,0:T(4,128)} %bitcast.32), channel_id=1, source_target_pairs={{0,20},{1,21},{2,22},{3,23},{4,16},{5,17},{6,18},{7,19},{8,28},{9,... | collective-permute-start | bytes 776 | tf_op jit(solution)/shard_map/ppermute | solution.py:418
  5.0 0.1 stack.23.refs_0_
  5.1 1.3 %prepare.1 = (bf16[32,1024]{1,0:T(8,128)(2,1)S(1)}, s32[1,4,16]{2,1,0:T(4,128)S(1)}) custom-call(s32[5]{0:T(128)S(1)} %stack.23.refs_0_, s32[1,4,16]{2,1,0:T(4,128)} %bitcast.33, f32[4,1024]{1,0:T(4,128)} %bitcast.30, s32[4,1024]{1,0:T(4,128)} %bitcast.31), custom_call_target="tpu_custom_call" | custom-call | flops 20000000000 | bytes 1024 | tf_op jit(solution)/shard_map/prepare/pallas_call | solution.py:74
  6.4 0.4 collective-permute-done.refs_1_
  6.8 4.8 %collective-permute-start.1 = (s32[2,4,16]{2,1,0:T(4,128)S(1)}, s32[2,4,16]{2,1,0:T(4,128)S(1)}, u32[]{:S(2)}, u32[]{:S(2)}) collective-permute-start(s32[2,4,16]{2,1,0:T(4,128)S(1)} %join.4.refs_1_.refs_2_), channel_id=1, source_target_pairs={{0,14},{1,15},{2,8},{3,9},{4,10},{5,11},{6,12},{7,13},{8,22},{9,23... | collective-permute-start | bytes 1544 | tf_op jit(solution)/shard_map/ppermute | solution.py:418
  11.6 0.0 copy-start
  11.6 0.0 copy-start.1
  11.6 2.6 %answer.3 = (bf16[1040,128]{1,0:T(8,128)(2,1)}, bf16[1040,128]{1,0:T(8,128)(2,1)}) custom-call(s32[5]{0:T(128)S(1)} %stack.23.refs_0_, s32[2,4,16]{2,1,0:T(4,128)S(1)} %join.4.refs_1_.refs_2_, s32[2,4,16]{2,1,0:T(4,128)S(1)} %join.4.refs_1_.refs_2_, bf16[32,1024]{1,0:T(8,128)(2,1)S(1)} %get-tuple-element.19.refs_3_.refs_5_.refs_6_, ...), custom_call_target="tpu_custom_call" | custom-call | flops 20000000000 | bytes 1024 | tf_op jit(solution)/shard_map/answer/pallas_call | solution.py:74
  14.2 0.1 collective-permute-start.6
  14.3 0.9 %collective-permute-start.7 = (bf16[1040,128]{1,0:T(8,128)(2,1)}, bf16[1040,128]{1,0:T(8,128)(2,1)}, u32[]{:S(2)}, u32[]{:S(2)}) collective-permute-start(bf16[1040,128]{1,0:T(8,128)(2,1)} %get-tuple-element.20.refs_3_.refs_6_), channel_id=1, source_target_pairs={{0,4},{1,5},{2,6},{3,7},{4,0},{5,1},{6,2},{7,3},{8,12},{9,13},{10,... | collective-permute-start | bytes 798728 | tf_op jit(solution)/shard_map/ppermute | solution.py:409
  15.2 0.0 collective-permute-done.1.refs_4_.refs_1_.refs_2_.refs_5_
  15.2 0.0 copy-done
  15.2 0.0 copy-done.1
  15.2 0.6 split.1
  15.9 1.9 %collective-permute-start.2 = (bf16[1,272,128]{2,1,0:T(8,128)(2,1)S(1)}, bf16[1,272,128]{2,1,0:T(8,128)(2,1)S(1)}, u32[]{:S(2)}, u32[]{:S(2)}) collective-permute-start(bf16[1,272,128]{2,1,0:T(8,128)(2,1)S(1)} %get-tuple-element.22), channel_id=1, source_target_pairs={{0,1},{1,0},{2,3},{3,2},{4,5},{5,4},{6,7},{7,6},{8,9},{9,8},{10,11... | collective-permute-start | bytes 208904 | tf_op jit(solution)/shard_map/ppermute | solution.py:409
  17.8 4.2 %own_blocks.1 = (f32[8,128,32,128]{3,2,1,0:T(8,128)S(1)}, bf16[1040,128]{1,0:T(8,128)(2,1)S(1)}) custom-call(s32[5]{0:T(128)S(1)} %stack.23.refs_0_, s32[1,4,16]{2,1,0:T(4,128)S(1)} %get-tuple-element.18.refs_0_.refs_1_.refs_2_, s32[1,4,16]{2,1,0:T(4,128)S(1)} %get-tuple-element.18.refs_0_.refs_1_.refs_2_, ...), custom_call_target="tpu_custom_call" | custom-call | flops 20000000000 | bytes 1024 | tf_op jit(solution)/shard_map/own_blocks/pallas_call | solution.py:74
  22.0 0.1 collective-permute-start.5
  22.1 1.6 %answer.4.refs_5_ = bf16[1040,128]{1,0:T(8,128)(2,1)S(1)} custom-call(s32[5]{0:T(128)S(1)} %stack.23.refs_0_, s32[2,4,16]{2,1,0:T(4,128)S(1)} %collective-permute-done.1.refs_4_.refs_1_.refs_2_.refs_5_, s32[2,4,16]{2,1,0:T(4,128)S(1)} %collective-permute-done.1.refs_4_.refs_1_.refs_2_.refs_5_, ...), custom_call_target="tpu_custom_call" | custom-call | flops 20000000000 | bytes 1024 | tf_op jit(solution)/shard_map/answer/pallas_call | solution.py:74
  23.7 0.1 collective-permute-start.8
  23.7 0.0 collective-permute-done.2.refs_1_
  23.8 1.6 %collective-permute-start.3 = (bf16[2,272,128]{2,1,0:T(8,128)(2,1)S(1)}, bf16[2,272,128]{2,1,0:T(8,128)(2,1)S(1)}, u32[]{:S(2)}, u32[]{:S(2)}) collective-permute-start(bf16[2,272,128]{2,1,0:T(8,128)(2,1)S(1)} %join.5.refs_0_.refs_1_), channel_id=1, source_target_pairs={{0,8},{8,0},{16,24},{24,16},{1,9},{9,1},{17,25},{25,17},{2,10},{10... | collective-permute-start | bytes 417800 | tf_op jit(solution)/shard_map/ppermute | solution.py:447
  25.3 1.6 %answer.5.refs_8_ = bf16[1040,128]{1,0:T(8,128)(2,1)S(1)} custom-call(s32[5]{0:T(128)S(1)} %stack.23.refs_0_, s32[2,4,16]{2,1,0:T(4,128)S(1)} %collective-permute-done.1.refs_4_.refs_1_.refs_2_.refs_5_, s32[2,4,16]{2,1,0:T(4,128)S(1)} %collective-permute-done.1.refs_4_.refs_1_.refs_2_.refs_5_, ...), custom_call_target="tpu_custom_call" | custom-call | flops 20000000000 | bytes 1024 | tf_op jit(solution)/shard_map/answer/pallas_call | solution.py:74
  26.9 3.0 %collective-permute-done.3.refs_1_ = bf16[2,272,128]{2,1,0:T(8,128)(2,1)S(1)} collective-permute-done((bf16[2,272,128]{2,1,0:T(8,128)(2,1)S(1)}, bf16[2,272,128]{2,1,0:T(8,128)(2,1)S(1)}, u32[]{:S(2)}, u32[]{:S(2)}) %collective-permute-start.3) | collective-permute-done | bytes 139296 | tf_op jit(solution)/shard_map/ppermute | solution.py:447
  29.9 0.0 collective-permute-start.9
  29.9 0.0 collective-permute-done.5.refs_3_
  30.0 1.6 %collective-permute-start.4 = (bf16[4,272,128]{2,1,0:T(8,128)(2,1)S(1)}, bf16[4,272,128]{2,1,0:T(8,128)(2,1)S(1)}, u32[]{:S(2)}, u32[]{:S(2)}) collective-permute-start(bf16[4,272,128]{2,1,0:T(8,128)(2,1)S(1)} %join.6.refs_0_), channel_id=1, source_target_pairs={{0,16},{8,24},{16,0},{24,8},{1,17},{9,25},{17,1},{25,9},{2,18},{10... | collective-permute-start | bytes 835592 | tf_op jit(solution)/shard_map/ppermute | solution.py:447
  31.5 2.6 %add_messages.5 = (f32[8,128,32,128]{3,2,1,0:T(8,128)S(1)}, bf16[1040,128]{1,0:T(8,128)(2,1)S(1)}) custom-call(s32[5]{0:T(128)S(1)} %stack.23.refs_0_, bf16[2,272,128]{2,1,0:T(8,128)(2,1)S(1)} %join.5.refs_0_.refs_1_, f32[8,128,32,128]{3,2,1,0:T(8,128)S(1)} %get-tuple-element.23.refs_2_, ...), custom_call_target="tpu_custom_call", output_to_operand_aliasing={{0}: (2, {})} | custom-call | flops 20000000000 | bytes 1024 | tf_op jit(solution)/shard_map/add_messages/pallas_call | solution.py:74
  34.1 5.1 %collective-permute-done.4.refs_1_ = bf16[4,272,128]{2,1,0:T(8,128)(2,1)S(1)} collective-permute-done((bf16[4,272,128]{2,1,0:T(8,128)(2,1)S(1)}, bf16[4,272,128]{2,1,0:T(8,128)(2,1)S(1)}, u32[]{:S(2)}, u32[]{:S(2)}) %collective-permute-start.4) | collective-permute-done | bytes 278560 | tf_op jit(solution)/shard_map/ppermute | solution.py:447
  39.2 3.3 %collective-permute-start.10 = (bf16[1040,128]{1,0:T(8,128)(2,1)S(1)}, bf16[1040,128]{1,0:T(8,128)(2,1)S(1)}, u32[]{:S(2)}, u32[]{:S(2)}) collective-permute-start(bf16[1040,128]{1,0:T(8,128)(2,1)S(1)} %get-tuple-element.27.refs_8_), channel_id=1, source_target_pairs={{0,6},{1,7},{2,0},{3,1},{4,2},{5,3},{6,4},{7,5},{8,14},{9,15},{10,... | collective-permute-start | bytes 798728 | tf_op jit(solution)/shard_map/ppermute | solution.py:409
  42.6 2.5 %collective-permute-done.6.refs_3_ = bf16[1040,128]{1,0:T(8,128)(2,1)} collective-permute-done((bf16[1040,128]{1,0:T(8,128)(2,1)}, bf16[1040,128]{1,0:T(8,128)(2,1)}, u32[]{:S(2)}, u32[]{:S(2)}) %collective-permute-start.6) | collective-permute-done | bytes 266272 | tf_op jit(solution)/shard_map/ppermute | solution.py:409
  45.1 2.9 %add_messages.6 = (f32[8,128,32,128]{3,2,1,0:T(8,128)S(1)}, bf16[1040,128]{1,0:T(8,128)(2,1)S(1)}) custom-call(s32[5]{0:T(128)S(1)} %stack.23.refs_0_, bf16[8,272,128]{2,1,0:T(8,128)(2,1)S(1)} %join.7.refs_1_, f32[8,128,32,128]{3,2,1,0:T(8,128)S(1)} %get-tuple-element.25.refs_2_, ...), custom_call_target="tpu_custom_call", output_to_operand_aliasing={{0}: (2, {})} | custom-call | flops 20000000000 | bytes 1024 | tf_op jit(solution)/shard_map/add_messages/pallas_call | solution.py:74
  48.0 0.2 collective-permute-start.11
  48.3 2.3 %collective-permute-done.7.refs_3_ = bf16[1040,128]{1,0:T(8,128)(2,1)} collective-permute-done((bf16[1040,128]{1,0:T(8,128)(2,1)}, bf16[1040,128]{1,0:T(8,128)(2,1)}, u32[]{:S(2)}, u32[]{:S(2)}) %collective-permute-start.7) | collective-permute-done | bytes 266272 | tf_op jit(solution)/shard_map/ppermute | solution.py:409
  50.6 2.6 %add_messages.7.refs_2_ = f32[8,128,32,128]{3,2,1,0:T(8,128)S(1)} custom-call(s32[5]{0:T(128)S(1)} %stack.23.refs_0_, bf16[8,272,128]{2,1,0:T(8,128)(2,1)S(1)} %join.7.refs_1_, f32[8,128,32,128]{3,2,1,0:T(8,128)S(1)} %get-tuple-element.28.refs_2_, bf16[1040,128]{1,0:T(8,128)(2,1)} %collective-permute-done.7.refs_3_), custom_call_target="tpu_custom_call", output_to_operand_aliasing={{}: (2, {})} | custom-call | flops 20000000000 | bytes 1024 | tf_op jit(solution)/shard_map/add_messages/pallas_call | solution.py:74
  53.2 0.0 collective-permute-done.8.refs_3_
  53.2 2.2 %add_messages.8.refs_2_ = f32[8,128,32,128]{3,2,1,0:T(8,128)S(1)} custom-call(s32[5]{0:T(128)S(1)} %stack.23.refs_0_, bf16[8,272,128]{2,1,0:T(8,128)(2,1)S(1)} %join.7.refs_1_, f32[8,128,32,128]{3,2,1,0:T(8,128)S(1)} %add_messages.7.refs_2_, bf16[1040,128]{1,0:T(8,128)(2,1)S(1)} %collective-permute-done.8.refs_3_), custom_call_target="tpu_custom_call", output_to_operand_aliasing={{}: (2, {})} | custom-call | flops 20000000000 | bytes 1024 | tf_op jit(solution)/shard_map/add_messages/pallas_call | solution.py:74
  55.5 0.0 collective-permute-done.9.refs_3_
  55.5 0.8 %collective-permute-done.10.refs_4_ = bf16[1040,128]{1,0:T(8,128)(2,1)S(1)} collective-permute-done((bf16[1040,128]{1,0:T(8,128)(2,1)S(1)}, bf16[1040,128]{1,0:T(8,128)(2,1)S(1)}, u32[]{:S(2)}, u32[]{:S(2)}) %collective-permute-start.10) | collective-permute-done | bytes 266272 | tf_op jit(solution)/shard_map/ppermute | solution.py:409
  56.3 5.5 %collective-permute-done.11.refs_5_ = bf16[1040,128]{1,0:T(8,128)(2,1)S(1)} collective-permute-done((bf16[1040,128]{1,0:T(8,128)(2,1)S(1)}, bf16[1040,128]{1,0:T(8,128)(2,1)S(1)}, u32[]{:S(2)}, u32[]{:S(2)}) %collective-permute-start.11) | collective-permute-done | bytes 266272 | tf_op jit(solution)/shard_map/ppermute | solution.py:409
  61.8 6.6 %add_messages.9 = (f32[8,128,32,128]{3,2,1,0:T(8,128)S(1)}, bf16[8,32,16384]{2,1,0:T(8,128)(2,1)}) custom-call(s32[5]{0:T(128)S(1)} %stack.23.refs_0_, bf16[8,272,128]{2,1,0:T(8,128)(2,1)S(1)} %join.7.refs_1_, f32[8,128,32,128]{3,2,1,0:T(8,128)S(1)} %add_messages.8.refs_2_, ...), custom_call_target="tpu_custom_call", output_to_operand_aliasing={{0}: (2, {})} | custom-call | flops 20000000000 | bytes 1024 | tf_op jit(solution)/shard_map/add_messages/pallas_call | solution.py:74
  (4 shorter events, 0.1 us)
Async XLA Ops:
  0.0 6.8 %collective-permute-start = (s32[1,4,16]{2,1,0:T(4,128)}, s32[1,4,16]{2,1,0:T(4,128)S(1)}, u32[]{:S(2)}, u32[]{:S(2)}) collective-permute-start(s32[1,4,16]{2,1,0:T(4,128)} %bitcast.32), channel_id=1, source_target_pairs={{0,20},{1,21},{2,22},{3,23},{4,16},{5,17},{6,18},{7,19},{8,28},{9,... | collective-permute-start | bytes 776 | tf_op jit(solution)/shard_map/ppermute | solution.py:418
  6.8 8.5 %collective-permute-start.1 = (s32[2,4,16]{2,1,0:T(4,128)S(1)}, s32[2,4,16]{2,1,0:T(4,128)S(1)}, u32[]{:S(2)}, u32[]{:S(2)}) collective-permute-start(s32[2,4,16]{2,1,0:T(4,128)S(1)} %join.4.refs_1_.refs_2_), channel_id=1, source_target_pairs={{0,14},{1,15},{2,8},{3,9},{4,10},{5,11},{6,12},{7,13},{8,22},{9,23... | collective-permute-start | bytes 1544 | tf_op jit(solution)/shard_map/ppermute | solution.py:418
  11.6 3.7 %copy-start = (bf16[1,1,16,32,128]{4,3,2,1,0:T(8,128)(2,1)S(1)}, bf16[1,1,16,32,128]{4,3,2,1,0:T(8,128)(2,1)}, u32[]{:S(2)}) copy-start(bf16[1,1,16,32,128]{4,3,2,1,0:T(8,128)(2,1)} %param.6) | copy-start | bytes 393220
  11.6 3.7 %copy-start.1 = (f32[1,1,16,4]{2,3,1,0:T(4,128)S(1)}, f32[1,1,16,4]{2,3,1,0:T(4,128)}, u32[]{:S(2)}) copy-start(f32[1,1,16,4]{2,3,1,0:T(4,128)} %param.7) | copy-start | bytes 772
  14.2 30.8 %collective-permute-start.6 = (bf16[1040,128]{1,0:T(8,128)(2,1)}, bf16[1040,128]{1,0:T(8,128)(2,1)}, u32[]{:S(2)}, u32[]{:S(2)}) collective-permute-start(bf16[1040,128]{1,0:T(8,128)(2,1)} %get-tuple-element.26), channel_id=1, source_target_pairs={{0,5},{1,4},{2,7},{3,6},{4,1},{5,0},{6,3},{7,2},{8,13},{9,12},{10,... | collective-permute-start | bytes 798728 | tf_op jit(solution)/shard_map/ppermute | solution.py:409
  14.3 36.3 %collective-permute-start.7 = (bf16[1040,128]{1,0:T(8,128)(2,1)}, bf16[1040,128]{1,0:T(8,128)(2,1)}, u32[]{:S(2)}, u32[]{:S(2)}) collective-permute-start(bf16[1040,128]{1,0:T(8,128)(2,1)} %get-tuple-element.20.refs_3_.refs_6_), channel_id=1, source_target_pairs={{0,4},{1,5},{2,6},{3,7},{4,0},{5,1},{6,2},{7,3},{8,12},{9,13},{10,... | collective-permute-start | bytes 798728 | tf_op jit(solution)/shard_map/ppermute | solution.py:409
  15.9 7.9 %collective-permute-start.2 = (bf16[1,272,128]{2,1,0:T(8,128)(2,1)S(1)}, bf16[1,272,128]{2,1,0:T(8,128)(2,1)S(1)}, u32[]{:S(2)}, u32[]{:S(2)}) collective-permute-start(bf16[1,272,128]{2,1,0:T(8,128)(2,1)S(1)} %get-tuple-element.22), channel_id=1, source_target_pairs={{0,1},{1,0},{2,3},{3,2},{4,5},{5,4},{6,7},{7,6},{8,9},{9,8},{10,11... | collective-permute-start | bytes 208904 | tf_op jit(solution)/shard_map/ppermute | solution.py:409
  22.0 7.9 %collective-permute-start.5 = (bf16[1040,128]{1,0:T(8,128)(2,1)S(1)}, bf16[1040,128]{1,0:T(8,128)(2,1)S(1)}, u32[]{:S(2)}, u32[]{:S(2)}) collective-permute-start(bf16[1040,128]{1,0:T(8,128)(2,1)S(1)} %get-tuple-element.24.refs_5_), channel_id=1, source_target_pairs={{0,1},{1,0},{2,3},{3,2},{4,5},{5,4},{6,7},{7,6},{8,9},{9,8},{10,11... | collective-permute-start | bytes 798728 | tf_op jit(solution)/shard_map/ppermute | solution.py:409
  23.7 29.6 %collective-permute-start.8 = (bf16[1040,128]{1,0:T(8,128)(2,1)S(1)}, bf16[1040,128]{1,0:T(8,128)(2,1)S(1)}, u32[]{:S(2)}, u32[]{:S(2)}) collective-permute-start(bf16[1040,128]{1,0:T(8,128)(2,1)S(1)} %answer.4.refs_5_), channel_id=1, source_target_pairs={{0,2},{1,3},{2,4},{3,5},{4,6},{5,7},{6,0},{7,1},{8,10},{9,11},{10,... | collective-permute-start | bytes 798728 | tf_op jit(solution)/shard_map/ppermute | solution.py:409
  23.8 6.1 %collective-permute-start.3 = (bf16[2,272,128]{2,1,0:T(8,128)(2,1)S(1)}, bf16[2,272,128]{2,1,0:T(8,128)(2,1)S(1)}, u32[]{:S(2)}, u32[]{:S(2)}) collective-permute-start(bf16[2,272,128]{2,1,0:T(8,128)(2,1)S(1)} %join.5.refs_0_.refs_1_), channel_id=1, source_target_pairs={{0,8},{8,0},{16,24},{24,16},{1,9},{9,1},{17,25},{25,17},{2,10},{10... | collective-permute-start | bytes 417800 | tf_op jit(solution)/shard_map/ppermute | solution.py:447
  29.9 25.6 %collective-permute-start.9 = (bf16[1040,128]{1,0:T(8,128)(2,1)S(1)}, bf16[1040,128]{1,0:T(8,128)(2,1)S(1)}, u32[]{:S(2)}, u32[]{:S(2)}) collective-permute-start(bf16[1040,128]{1,0:T(8,128)(2,1)S(1)} %answer.5.refs_8_), channel_id=1, source_target_pairs={{0,3},{1,2},{2,5},{3,4},{4,7},{5,6},{6,1},{7,0},{8,11},{9,10},{10,... | collective-permute-start | bytes 798728 | tf_op jit(solution)/shard_map/ppermute | solution.py:409
  30.0 9.3 %collective-permute-start.4 = (bf16[4,272,128]{2,1,0:T(8,128)(2,1)S(1)}, bf16[4,272,128]{2,1,0:T(8,128)(2,1)S(1)}, u32[]{:S(2)}, u32[]{:S(2)}) collective-permute-start(bf16[4,272,128]{2,1,0:T(8,128)(2,1)S(1)} %join.6.refs_0_), channel_id=1, source_target_pairs={{0,16},{8,24},{16,0},{24,8},{1,17},{9,25},{17,1},{25,9},{2,18},{10... | collective-permute-start | bytes 835592 | tf_op jit(solution)/shard_map/ppermute | solution.py:447
  39.2 17.1 %collective-permute-start.10 = (bf16[1040,128]{1,0:T(8,128)(2,1)S(1)}, bf16[1040,128]{1,0:T(8,128)(2,1)S(1)}, u32[]{:S(2)}, u32[]{:S(2)}) collective-permute-start(bf16[1040,128]{1,0:T(8,128)(2,1)S(1)} %get-tuple-element.27.refs_8_), channel_id=1, source_target_pairs={{0,6},{1,7},{2,0},{3,1},{4,2},{5,3},{6,4},{7,5},{8,14},{9,15},{10,... | collective-permute-start | bytes 798728 | tf_op jit(solution)/shard_map/ppermute | solution.py:409
  48.0 13.8 %collective-permute-start.11 = (bf16[1040,128]{1,0:T(8,128)(2,1)S(1)}, bf16[1040,128]{1,0:T(8,128)(2,1)S(1)}, u32[]{:S(2)}, u32[]{:S(2)}) collective-permute-start(bf16[1040,128]{1,0:T(8,128)(2,1)S(1)} %get-tuple-element.29), channel_id=1, source_target_pairs={{0,7},{1,6},{2,1},{3,0},{4,3},{5,2},{6,5},{7,4},{8,15},{9,14},{10,... | collective-permute-start | bytes 798728 | tf_op jit(solution)/shard_map/ppermute | solution.py:409

commit v2 on v1

--- a/solution.py
+++ b/solution.py
@@ -460,19 +460,16 @@
         z, info, own_left, [(0, 1, taken)], mine.acc, (*asked[last], 0, table, b_part), after=after
     )
     acc, ends = got.acc, [got.message]
+    ends.append(answer(z, info, *asked[last], (1,), table, b_part, ends[0]).m1)
     early = [(by, flip) for by in order[:-1] for flip in range(halves)]
     early[:halves] = early[halves - 1 :: -1]
-    for at, (by, flip) in enumerate(early[:-1]):
-        got = add_messages(
-            z, info, left, [(by, flip, moving[by, flip])], acc,
-            (*asked[last], 1, table, b_part) if at == 0 else None, after=ends[0] if at == 0 else None,
-        )
-        acc = got.acc
-        if at == 0:
-            ends.append(got.message)
-    final = [(*early[-1], moving[early[-1]])]
-    final += [(last, flip, step(ends[flip], last, flip)) for flip in range(halves)]
-    out = add_messages(z, info, left, final, acc, write=True).out
+    after = ends[1]
+    for by, flip in early[:-1]:
+        acc = add_messages(z, info, left, [(by, flip, moving[by, flip])], acc, after=after).acc
+        after = None
+    both = [(*early[-1], moving[early[-1]]), (last, 0, step(ends[0], last, 0))]
+    acc = add_messages(z, info, left, both, acc).acc
+    out = add_messages(z, info, left, [(last, 1, step(ends[1], last, 1))], acc, write=True).out
     return out[None, None]
 
 

time: 69.1 us -> 67.9 us (0.983)
  waiting for transfers between devices: 19.7 us -> 14.2 us
  Pallas kernels: 29 us -> 33.5 us
    pallas_call x15 -> x17, Pallas kernels: 29 us -> 33.5 us  [kernel_call(): pl.pallas_call(kernel, out_shape=list(outs.values()), in_specs=[pl.BlockS...]
    ppermute x8, waiting for transfers between devices: 11.2 us -> 7.32 us  [step(): return lax.ppermute(value, COL, pairs)]
    ppermute x2, waiting for transfers between devices: 8.13 us -> 6.54 us  [on_device(): lax.ppermute(left, ROW, [(r, r ^ bit) for r in range(panels)])]
  transfers between devices with their start and end apart: 12 -> 12, of which waited for: 7 -> 7; matrix products, arithmetic and copies ran while one was open for 0% -> 0% of each run, Pallas kernels for 33% -> 42%
where the time goes in v2:
time: 67.9 us; the launch traced here: 67.4 us
  Pallas kernels  33.5 us (49%)
  starting transfers between devices  19.3 us (28%)
  waiting for transfers between devices  14.2 us (21%)
    pallas_call x17, Pallas kernels, kernel_call(): pl.pallas_call(kernel, out_shape=list(outs.values()), in_specs=[pl.BlockS...  33.5 us
    ppermute x2, starting transfers between devices, named_by(): return lax.ppermute(cols, (ROW, COL), pairs)  9.8 us
    ppermute x8, waiting for transfers between devices, step(): return lax.ppermute(value, COL, pairs)  7.32 us
    ppermute x2, waiting for transfers between devices, on_device(): lax.ppermute(left, ROW, [(r, r ^ bit) for r in range(panels)])  6.54 us
    ppermute x8, starting transfers between devices, step(): return lax.ppermute(value, COL, pairs)  6.32 us
    ppermute x2, starting transfers between devices, on_device(): lax.ppermute(left, ROW, [(r, r ^ bit) for r in range(panels)])  3.14 us
  transfers between devices with their start and end apart: 12, of which 7 were waited for; matrix products, arithmetic and copies ran while one was open for 0% of the time, Pallas kernels for 42%

profile of v2, /device:TPU:0, one launch (start us, length us, event | category | flops | bytes accessed | tf_op | source)
XLA Modules:
  0.0 67.4 jit_solution(8883001076132526984)
XLA Ops:
  0.0 5.0 %collective-permute-start = (s32[1,4,16]{2,1,0:T(4,128)}, s32[1,4,16]{2,1,0:T(4,128)S(1)}, u32[]{:S(2)}, u32[]{:S(2)}) collective-permute-start(s32[1,4,16]{2,1,0:T(4,128)} %bitcast.32), channel_id=1, source_target_pairs={{0,20},{1,21},{2,22},{3,23},{4,16},{5,17},{6,18},{7,19},{8,28},{9,... | collective-permute-start | bytes 776 | tf_op jit(solution)/shard_map/ppermute | solution.py:418
  5.0 0.1 stack.23.refs_0_
  5.1 1.3 %prepare.1 = (bf16[32,1024]{1,0:T(8,128)(2,1)S(1)}, s32[1,4,16]{2,1,0:T(4,128)S(1)}) custom-call(s32[5]{0:T(128)S(1)} %stack.23.refs_0_, s32[1,4,16]{2,1,0:T(4,128)} %bitcast.33, f32[4,1024]{1,0:T(4,128)} %bitcast.30, s32[4,1024]{1,0:T(4,128)} %bitcast.31), custom_call_target="tpu_custom_call" | custom-call | flops 20000000000 | bytes 1024 | tf_op jit(solution)/shard_map/prepare/pallas_call | solution.py:74
  6.4 0.4 collective-permute-done.refs_1_
  6.8 4.8 %collective-permute-start.1 = (s32[2,4,16]{2,1,0:T(4,128)S(1)}, s32[2,4,16]{2,1,0:T(4,128)S(1)}, u32[]{:S(2)}, u32[]{:S(2)}) collective-permute-start(s32[2,4,16]{2,1,0:T(4,128)S(1)} %join.4.refs_1_.refs_2_), channel_id=1, source_target_pairs={{0,14},{1,15},{2,8},{3,9},{4,10},{5,11},{6,12},{7,13},{8,22},{9,23... | collective-permute-start | bytes 1544 | tf_op jit(solution)/shard_map/ppermute | solution.py:418
  11.6 0.0 copy-start
  11.6 0.0 copy-start.1
  11.6 2.6 %answer.4 = (bf16[1040,128]{1,0:T(8,128)(2,1)}, bf16[1040,128]{1,0:T(8,128)(2,1)}) custom-call(s32[5]{0:T(128)S(1)} %stack.23.refs_0_, s32[2,4,16]{2,1,0:T(4,128)S(1)} %join.4.refs_1_.refs_2_, s32[2,4,16]{2,1,0:T(4,128)S(1)} %join.4.refs_1_.refs_2_, bf16[32,1024]{1,0:T(8,128)(2,1)S(1)} %get-tuple-element.17.refs_3_.refs_5_.refs_6_, ...), custom_call_target="tpu_custom_call" | custom-call | flops 20000000000 | bytes 1024 | tf_op jit(solution)/shard_map/answer/pallas_call | solution.py:74
  14.2 0.1 collective-permute-start.6
  14.3 0.9 %collective-permute-start.7 = (bf16[1040,128]{1,0:T(8,128)(2,1)}, bf16[1040,128]{1,0:T(8,128)(2,1)}, u32[]{:S(2)}, u32[]{:S(2)}) collective-permute-start(bf16[1040,128]{1,0:T(8,128)(2,1)} %get-tuple-element.18.refs_3_.refs_6_), channel_id=1, source_target_pairs={{0,4},{1,5},{2,6},{3,7},{4,0},{5,1},{6,2},{7,3},{8,12},{9,13},{10,... | collective-permute-start | bytes 798728 | tf_op jit(solution)/shard_map/ppermute | solution.py:409
  15.2 0.0 collective-permute-done.1.refs_4_.refs_1_.refs_2_.refs_5_
  15.2 0.0 copy-done
  15.2 0.0 copy-done.1
  15.2 0.6 split.1
  15.9 1.9 %collective-permute-start.2 = (bf16[1,272,128]{2,1,0:T(8,128)(2,1)S(1)}, bf16[1,272,128]{2,1,0:T(8,128)(2,1)S(1)}, u32[]{:S(2)}, u32[]{:S(2)}) collective-permute-start(bf16[1,272,128]{2,1,0:T(8,128)(2,1)S(1)} %get-tuple-element.20), channel_id=1, source_target_pairs={{0,1},{1,0},{2,3},{3,2},{4,5},{5,4},{6,7},{7,6},{8,9},{9,8},{10,11... | collective-permute-start | bytes 208904 | tf_op jit(solution)/shard_map/ppermute | solution.py:409
  17.8 4.2 %own_blocks.1 = (f32[8,128,32,128]{3,2,1,0:T(8,128)S(1)}, bf16[1040,128]{1,0:T(8,128)(2,1)S(1)}) custom-call(s32[5]{0:T(128)S(1)} %stack.23.refs_0_, s32[1,4,16]{2,1,0:T(4,128)S(1)} %get-tuple-element.16.refs_0_.refs_1_.refs_2_, s32[1,4,16]{2,1,0:T(4,128)S(1)} %get-tuple-element.16.refs_0_.refs_1_.refs_2_, ...), custom_call_target="tpu_custom_call" | custom-call | flops 20000000000 | bytes 1024 | tf_op jit(solution)/shard_map/own_blocks/pallas_call | solution.py:74
  22.0 0.1 collective-permute-start.5
  22.1 2.3 %answer.5.refs_5_ = bf16[1040,128]{1,0:T(8,128)(2,1)} custom-call(s32[5]{0:T(128)S(1)} %stack.23.refs_0_, s32[2,4,16]{2,1,0:T(4,128)S(1)} %collective-permute-done.1.refs_4_.refs_1_.refs_2_.refs_5_, s32[2,4,16]{2,1,0:T(4,128)S(1)} %collective-permute-done.1.refs_4_.refs_1_.refs_2_.refs_5_, bf16[32,1024]{1,0:T(8,128)(2,1)S(1)} %get-tuple-element.17.refs_3_.refs_5_.refs_6_, ...), custom_call_target="tpu_custom_call" | custom-call | flops 20000000000 | bytes 1024 | tf_op jit(solution)/shard_map/answer/pallas_call | solution.py:74
  24.4 0.1 collective-permute-start.8
  24.5 0.0 collective-permute-done.2.refs_1_
  24.5 1.6 %collective-permute-start.3 = (bf16[2,272,128]{2,1,0:T(8,128)(2,1)S(1)}, bf16[2,272,128]{2,1,0:T(8,128)(2,1)S(1)}, u32[]{:S(2)}, u32[]{:S(2)}) collective-permute-start(bf16[2,272,128]{2,1,0:T(8,128)(2,1)S(1)} %join.5.refs_0_.refs_1_), channel_id=1, source_target_pairs={{0,8},{8,0},{16,24},{24,16},{1,9},{9,1},{17,25},{25,17},{2,10},{10... | collective-permute-start | bytes 417800 | tf_op jit(solution)/shard_map/ppermute | solution.py:447
  26.0 1.6 %answer.6.refs_8_ = bf16[1040,128]{1,0:T(8,128)(2,1)S(1)} custom-call(s32[5]{0:T(128)S(1)} %stack.23.refs_0_, s32[2,4,16]{2,1,0:T(4,128)S(1)} %collective-permute-done.1.refs_4_.refs_1_.refs_2_.refs_5_, s32[2,4,16]{2,1,0:T(4,128)S(1)} %collective-permute-done.1.refs_4_.refs_1_.refs_2_.refs_5_, ...), custom_call_target="tpu_custom_call" | custom-call | flops 20000000000 | bytes 1024 | tf_op jit(solution)/shard_map/answer/pallas_call | solution.py:74
  27.6 3.0 %collective-permute-done.3.refs_1_ = bf16[2,272,128]{2,1,0:T(8,128)(2,1)S(1)} collective-permute-done((bf16[2,272,128]{2,1,0:T(8,128)(2,1)S(1)}, bf16[2,272,128]{2,1,0:T(8,128)(2,1)S(1)}, u32[]{:S(2)}, u32[]{:S(2)}) %collective-permute-start.3) | collective-permute-done | bytes 139296 | tf_op jit(solution)/shard_map/ppermute | solution.py:447
  30.6 0.0 collective-permute-start.9
  30.6 0.0 collective-permute-done.5.refs_3_
  30.7 1.6 %collective-permute-start.4 = (bf16[4,272,128]{2,1,0:T(8,128)(2,1)S(1)}, bf16[4,272,128]{2,1,0:T(8,128)(2,1)S(1)}, u32[]{:S(2)}, u32[]{:S(2)}) collective-permute-start(bf16[4,272,128]{2,1,0:T(8,128)(2,1)S(1)} %join.6.refs_0_), channel_id=1, source_target_pairs={{0,16},{8,24},{16,0},{24,8},{1,17},{9,25},{17,1},{25,9},{2,18},{10... | collective-permute-start | bytes 835592 | tf_op jit(solution)/shard_map/ppermute | solution.py:447
  32.2 2.6 %add_messages.6 = (f32[8,128,32,128]{3,2,1,0:T(8,128)S(1)}, bf16[1040,128]{1,0:T(8,128)(2,1)S(1)}) custom-call(s32[5]{0:T(128)S(1)} %stack.23.refs_0_, bf16[2,272,128]{2,1,0:T(8,128)(2,1)S(1)} %join.5.refs_0_.refs_1_, f32[8,128,32,128]{3,2,1,0:T(8,128)S(1)} %get-tuple-element.21.refs_2_, ...), custom_call_target="tpu_custom_call", output_to_operand_aliasing={{0}: (2, {})} | custom-call | flops 20000000000 | bytes 1024 | tf_op jit(solution)/shard_map/add_messages/pallas_call | solution.py:74
  34.8 1.6 %answer.7.refs_4_ = bf16[1040,128]{1,0:T(8,128)(2,1)S(1)} custom-call(s32[5]{0:T(128)S(1)} %stack.23.refs_0_, s32[2,4,16]{2,1,0:T(4,128)S(1)} %collective-permute-done.1.refs_4_.refs_1_.refs_2_.refs_5_, s32[2,4,16]{2,1,0:T(4,128)S(1)} %collective-permute-done.1.refs_4_.refs_1_.refs_2_.refs_5_, ...), custom_call_target="tpu_custom_call" | custom-call | flops 20000000000 | bytes 1024 | tf_op jit(solution)/shard_map/answer/pallas_call | solution.py:74
  36.4 3.5 %collective-permute-done.4.refs_1_ = bf16[4,272,128]{2,1,0:T(8,128)(2,1)S(1)} collective-permute-done((bf16[4,272,128]{2,1,0:T(8,128)(2,1)S(1)}, bf16[4,272,128]{2,1,0:T(8,128)(2,1)S(1)}, u32[]{:S(2)}, u32[]{:S(2)}) %collective-permute-start.4) | collective-permute-done | bytes 278560 | tf_op jit(solution)/shard_map/ppermute | solution.py:447
  39.9 3.3 %collective-permute-start.10 = (bf16[1040,128]{1,0:T(8,128)(2,1)S(1)}, bf16[1040,128]{1,0:T(8,128)(2,1)S(1)}, u32[]{:S(2)}, u32[]{:S(2)}) collective-permute-start(bf16[1040,128]{1,0:T(8,128)(2,1)S(1)} %get-tuple-element.25.refs_5_), channel_id=1, source_target_pairs={{0,6},{1,7},{2,0},{3,1},{4,2},{5,3},{6,4},{7,5},{8,14},{9,15},{10,... | collective-permute-start | bytes 798728 | tf_op jit(solution)/shard_map/ppermute | solution.py:409
  43.3 1.8 %collective-permute-done.6.refs_3_ = bf16[1040,128]{1,0:T(8,128)(2,1)} collective-permute-done((bf16[1040,128]{1,0:T(8,128)(2,1)}, bf16[1040,128]{1,0:T(8,128)(2,1)}, u32[]{:S(2)}, u32[]{:S(2)}) %collective-permute-start.6) | collective-permute-done | bytes 266272 | tf_op jit(solution)/shard_map/ppermute | solution.py:409
  45.1 0.0 collective-permute-start.11
  45.1 2.6 %add_messages.7.refs_2_ = f32[8,128,32,128]{3,2,1,0:T(8,128)S(1)} custom-call(s32[5]{0:T(128)S(1)} %stack.23.refs_0_, bf16[8,272,128]{2,1,0:T(8,128)(2,1)S(1)} %join.7.refs_1_, f32[8,128,32,128]{3,2,1,0:T(8,128)S(1)} %get-tuple-element.23.refs_2_, bf16[1040,128]{1,0:T(8,128)(2,1)} %collective-permute-done.6.refs_3_, ...), custom_call_target="tpu_custom_call", output_to_operand_aliasing={{}: (2, {})} | custom-call | flops 20000000000 | bytes 1024 | tf_op jit(solution)/shard_map/add_messages/pallas_call | solution.py:74
  47.7 2.9 %collective-permute-done.7.refs_3_ = bf16[1040,128]{1,0:T(8,128)(2,1)} collective-permute-done((bf16[1040,128]{1,0:T(8,128)(2,1)}, bf16[1040,128]{1,0:T(8,128)(2,1)}, u32[]{:S(2)}, u32[]{:S(2)}) %collective-permute-start.7) | collective-permute-done | bytes 266272 | tf_op jit(solution)/shard_map/ppermute | solution.py:409
  50.6 2.6 %add_messages.8.refs_2_ = f32[8,128,32,128]{3,2,1,0:T(8,128)S(1)} custom-call(s32[5]{0:T(128)S(1)} %stack.23.refs_0_, bf16[8,272,128]{2,1,0:T(8,128)(2,1)S(1)} %join.7.refs_1_, f32[8,128,32,128]{3,2,1,0:T(8,128)S(1)} %add_messages.7.refs_2_, bf16[1040,128]{1,0:T(8,128)(2,1)} %collective-permute-done.7.refs_3_), custom_call_target="tpu_custom_call", output_to_operand_aliasing={{}: (2, {})} | custom-call | flops 20000000000 | bytes 1024 | tf_op jit(solution)/shard_map/add_messages/pallas_call | solution.py:74
  53.2 0.0 collective-permute-done.8.refs_3_
  53.2 2.6 %add_messages.9.refs_2_ = f32[8,128,32,128]{3,2,1,0:T(8,128)S(1)} custom-call(s32[5]{0:T(128)S(1)} %stack.23.refs_0_, bf16[8,272,128]{2,1,0:T(8,128)(2,1)S(1)} %join.7.refs_1_, f32[8,128,32,128]{3,2,1,0:T(8,128)S(1)} %add_messages.8.refs_2_, bf16[1040,128]{1,0:T(8,128)(2,1)} %collective-permute-done.8.refs_3_), custom_call_target="tpu_custom_call", output_to_operand_aliasing={{}: (2, {})} | custom-call | flops 20000000000 | bytes 1024 | tf_op jit(solution)/shard_map/add_messages/pallas_call | solution.py:74
  55.9 0.0 collective-permute-done.9.refs_3_
  55.9 0.4 collective-permute-done.10.refs_4_
  56.3 3.3 %add_messages.10.refs_2_ = f32[8,128,32,128]{3,2,1,0:T(8,128)S(1)} custom-call(s32[5]{0:T(128)S(1)} %stack.23.refs_0_, bf16[8,272,128]{2,1,0:T(8,128)(2,1)S(1)} %join.7.refs_1_, f32[8,128,32,128]{3,2,1,0:T(8,128)S(1)} %add_messages.9.refs_2_, bf16[1040,128]{1,0:T(8,128)(2,1)S(1)} %collective-permute-done.9.refs_3_, ...), custom_call_target="tpu_custom_call", output_to_operand_aliasing={{}: (2, {})} | custom-call | flops 20000000000 | bytes 1024 | tf_op jit(solution)/shard_map/add_messages/pallas_call | solution.py:74
  59.5 2.3 %collective-permute-done.11.refs_3_ = bf16[1040,128]{1,0:T(8,128)(2,1)S(1)} collective-permute-done((bf16[1040,128]{1,0:T(8,128)(2,1)S(1)}, bf16[1040,128]{1,0:T(8,128)(2,1)S(1)}, u32[]{:S(2)}, u32[]{:S(2)}) %collective-permute-start.11) | collective-permute-done | bytes 266272 | tf_op jit(solution)/shard_map/ppermute | solution.py:409
  61.8 5.5 %add_messages.11 = (f32[8,128,32,128]{3,2,1,0:T(8,128)S(1)}, bf16[8,32,16384]{2,1,0:T(8,128)(2,1)}) custom-call(s32[5]{0:T(128)S(1)} %stack.23.refs_0_, bf16[8,272,128]{2,1,0:T(8,128)(2,1)S(1)} %join.7.refs_1_, f32[8,128,32,128]{3,2,1,0:T(8,128)S(1)} %add_messages.10.refs_2_, ...), custom_call_target="tpu_custom_call", output_to_operand_aliasing={{0}: (2, {})} | custom-call | flops 20000000000 | bytes 1024 | tf_op jit(solution)/shard_map/add_messages/pallas_call | solution.py:74
  (4 shorter events, 0.1 us)
Async XLA Ops:
  0.0 6.8 %collective-permute-start = (s32[1,4,16]{2,1,0:T(4,128)}, s32[1,4,16]{2,1,0:T(4,128)S(1)}, u32[]{:S(2)}, u32[]{:S(2)}) collective-permute-start(s32[1,4,16]{2,1,0:T(4,128)} %bitcast.32), channel_id=1, source_target_pairs={{0,20},{1,21},{2,22},{3,23},{4,16},{5,17},{6,18},{7,19},{8,28},{9,... | collective-permute-start | bytes 776 | tf_op jit(solution)/shard_map/ppermute | solution.py:418
  6.8 8.5 %collective-permute-start.1 = (s32[2,4,16]{2,1,0:T(4,128)S(1)}, s32[2,4,16]{2,1,0:T(4,128)S(1)}, u32[]{:S(2)}, u32[]{:S(2)}) collective-permute-start(s32[2,4,16]{2,1,0:T(4,128)S(1)} %join.4.refs_1_.refs_2_), channel_id=1, source_target_pairs={{0,14},{1,15},{2,8},{3,9},{4,10},{5,11},{6,12},{7,13},{8,22},{9,23... | collective-permute-start | bytes 1544 | tf_op jit(solution)/shard_map/ppermute | solution.py:418
  11.6 3.7 %copy-start = (bf16[1,1,16,32,128]{4,3,2,1,0:T(8,128)(2,1)S(1)}, bf16[1,1,16,32,128]{4,3,2,1,0:T(8,128)(2,1)}, u32[]{:S(2)}) copy-start(bf16[1,1,16,32,128]{4,3,2,1,0:T(8,128)(2,1)} %param.6) | copy-start | bytes 393220
  11.6 3.7 %copy-start.1 = (f32[1,1,16,4]{2,3,1,0:T(4,128)S(1)}, f32[1,1,16,4]{2,3,1,0:T(4,128)}, u32[]{:S(2)}) copy-start(f32[1,1,16,4]{2,3,1,0:T(4,128)} %param.7) | copy-start | bytes 772
  14.2 30.8 %collective-permute-start.6 = (bf16[1040,128]{1,0:T(8,128)(2,1)}, bf16[1040,128]{1,0:T(8,128)(2,1)}, u32[]{:S(2)}, u32[]{:S(2)}) collective-permute-start(bf16[1040,128]{1,0:T(8,128)(2,1)} %get-tuple-element.24), channel_id=1, source_target_pairs={{0,5},{1,4},{2,7},{3,6},{4,1},{5,0},{6,3},{7,2},{8,13},{9,12},{10,... | collective-permute-start | bytes 798728 | tf_op jit(solution)/shard_map/ppermute | solution.py:409
  14.3 36.3 %collective-permute-start.7 = (bf16[1040,128]{1,0:T(8,128)(2,1)}, bf16[1040,128]{1,0:T(8,128)(2,1)}, u32[]{:S(2)}, u32[]{:S(2)}) collective-permute-start(bf16[1040,128]{1,0:T(8,128)(2,1)} %get-tuple-element.18.refs_3_.refs_6_), channel_id=1, source_target_pairs={{0,4},{1,5},{2,6},{3,7},{4,0},{5,1},{6,2},{7,3},{8,12},{9,13},{10,... | collective-permute-start | bytes 798728 | tf_op jit(solution)/shard_map/ppermute | solution.py:409
  15.9 8.6 %collective-permute-start.2 = (bf16[1,272,128]{2,1,0:T(8,128)(2,1)S(1)}, bf16[1,272,128]{2,1,0:T(8,128)(2,1)S(1)}, u32[]{:S(2)}, u32[]{:S(2)}) collective-permute-start(bf16[1,272,128]{2,1,0:T(8,128)(2,1)S(1)} %get-tuple-element.20), channel_id=1, source_target_pairs={{0,1},{1,0},{2,3},{3,2},{4,5},{5,4},{6,7},{7,6},{8,9},{9,8},{10,11... | collective-permute-start | bytes 208904 | tf_op jit(solution)/shard_map/ppermute | solution.py:409
  22.0 8.6 %collective-permute-start.5 = (bf16[1040,128]{1,0:T(8,128)(2,1)S(1)}, bf16[1040,128]{1,0:T(8,128)(2,1)S(1)}, u32[]{:S(2)}, u32[]{:S(2)}) collective-permute-start(bf16[1040,128]{1,0:T(8,128)(2,1)S(1)} %get-tuple-element.22.refs_5_), channel_id=1, source_target_pairs={{0,1},{1,0},{2,3},{3,2},{4,5},{5,4},{6,7},{7,6},{8,9},{9,8},{10,11... | collective-permute-start | bytes 798728 | tf_op jit(solution)/shard_map/ppermute | solution.py:409
  24.4 28.8 %collective-permute-start.8 = (bf16[1040,128]{1,0:T(8,128)(2,1)}, bf16[1040,128]{1,0:T(8,128)(2,1)}, u32[]{:S(2)}, u32[]{:S(2)}) collective-permute-start(bf16[1040,128]{1,0:T(8,128)(2,1)} %answer.5.refs_5_), channel_id=1, source_target_pairs={{0,2},{1,3},{2,4},{3,5},{4,6},{5,7},{6,0},{7,1},{8,10},{9,11},{10,... | collective-permute-start | bytes 798728 | tf_op jit(solution)/shard_map/ppermute | solution.py:409
  24.5 6.1 %collective-permute-start.3 = (bf16[2,272,128]{2,1,0:T(8,128)(2,1)S(1)}, bf16[2,272,128]{2,1,0:T(8,128)(2,1)S(1)}, u32[]{:S(2)}, u32[]{:S(2)}) collective-permute-start(bf16[2,272,128]{2,1,0:T(8,128)(2,1)S(1)} %join.5.refs_0_.refs_1_), channel_id=1, source_target_pairs={{0,8},{8,0},{16,24},{24,16},{1,9},{9,1},{17,25},{25,17},{2,10},{10... | collective-permute-start | bytes 417800 | tf_op jit(solution)/shard_map/ppermute | solution.py:447
  30.6 25.3 %collective-permute-start.9 = (bf16[1040,128]{1,0:T(8,128)(2,1)S(1)}, bf16[1040,128]{1,0:T(8,128)(2,1)S(1)}, u32[]{:S(2)}, u32[]{:S(2)}) collective-permute-start(bf16[1040,128]{1,0:T(8,128)(2,1)S(1)} %answer.6.refs_8_), channel_id=1, source_target_pairs={{0,3},{1,2},{2,5},{3,4},{4,7},{5,6},{6,1},{7,0},{8,11},{9,10},{10,... | collective-permute-start | bytes 798728 | tf_op jit(solution)/shard_map/ppermute | solution.py:409
  30.7 9.3 %collective-permute-start.4 = (bf16[4,272,128]{2,1,0:T(8,128)(2,1)S(1)}, bf16[4,272,128]{2,1,0:T(8,128)(2,1)S(1)}, u32[]{:S(2)}, u32[]{:S(2)}) collective-permute-start(bf16[4,272,128]{2,1,0:T(8,128)(2,1)S(1)} %join.6.refs_0_), channel_id=1, source_target_pairs={{0,16},{8,24},{16,0},{24,8},{1,17},{9,25},{17,1},{25,9},{2,18},{10... | collective-permute-start | bytes 835592 | tf_op jit(solution)/shard_map/ppermute | solution.py:447
  39.9 16.3 %collective-permute-start.10 = (bf16[1040,128]{1,0:T(8,128)(2,1)S(1)}, bf16[1040,128]{1,0:T(8,128)(2,1)S(1)}, u32[]{:S(2)}, u32[]{:S(2)}) collective-permute-start(bf16[1040,128]{1,0:T(8,128)(2,1)S(1)} %get-tuple-element.25.refs_5_), channel_id=1, source_target_pairs={{0,6},{1,7},{2,0},{3,1},{4,2},{5,3},{6,4},{7,5},{8,14},{9,15},{10,... | collective-permute-start | bytes 798728 | tf_op jit(solution)/shard_map/ppermute | solution.py:409
  45.1 16.7 %collective-permute-start.11 = (bf16[1040,128]{1,0:T(8,128)(2,1)S(1)}, bf16[1040,128]{1,0:T(8,128)(2,1)S(1)}, u32[]{:S(2)}, u32[]{:S(2)}) collective-permute-start(bf16[1040,128]{1,0:T(8,128)(2,1)S(1)} %answer.7.refs_4_), channel_id=1, source_target_pairs={{0,7},{1,6},{2,1},{3,0},{4,3},{5,2},{6,5},{7,4},{8,15},{9,14},{10,... | collective-permute-start | bytes 798728 | tf_op jit(solution)/shard_map/ppermute | solution.py:409

commit v3 on v2

--- a/solution.py
+++ b/solution.py
@@ -447,17 +447,16 @@
         left = join(left, lax.ppermute(left, ROW, [(r, r ^ bit) for r in range(panels)]))
         bit *= 2
 
-    mine = own_blocks(z, info, own_cols, table, b_part, pieces.kept, after)
-    taken = step(mine.message, 0, 1)
-    after = mine.message
     for by in order[1:-1]:
         for flip in range(halves):
             got = answer(z, info, *asked[by], (flip,), table, b_part, after)
             (after,) = vars(got).values()
             moving[by, flip] = step(after, by, flip)
+    mine = own_blocks(z, info, own_cols, table, b_part, pieces.kept, after)
+    taken = step(mine.message, 0, 1)
 
     got = add_messages(
-        z, info, own_left, [(0, 1, taken)], mine.acc, (*asked[last], 0, table, b_part), after=after
+        z, info, own_left, [(0, 1, taken)], mine.acc, (*asked[last], 0, table, b_part)
     )
     acc, ends = got.acc, [got.message]
     ends.append(answer(z, info, *asked[last], (1,), table, b_part, ends[0]).m1)

time: 67.9 us -> 68.1 us (level)
  waiting for transfers between devices: 14.2 us -> 12.8 us
  Pallas kernels: 33.5 us -> 34.6 us
    ppermute x2, waiting for transfers between devices: 6.54 us -> 3.2 us  [on_device(): lax.ppermute(left, ROW, [(r, r ^ bit) for r in range(panels)])]
    ppermute x8, waiting for transfers between devices: 7.32 us -> 9.2 us  [step(): return lax.ppermute(value, COL, pairs)]
    pallas_call x17, Pallas kernels: 33.5 us -> 34.6 us  [kernel_call(): pl.pallas_call(kernel, out_shape=list(outs.values()), in_specs=[pl.BlockS...]
  transfers between devices with their start and end apart: 12 -> 12, of which waited for: 7 -> 8; matrix products, arithmetic and copies ran while one was open for 0% -> 0% of each run, Pallas kernels for 42% -> 43%
where the time goes in v3:
time: 68.1 us; the launch traced here: 67.4 us
  Pallas kernels  34.6 us (51%)
  starting transfers between devices  19.6 us (29%)
  waiting for transfers between devices  12.8 us (19%)
    pallas_call x17, Pallas kernels, kernel_call(): pl.pallas_call(kernel, out_shape=list(outs.values()), in_specs=[pl.BlockS...  34.6 us
    ppermute x2, starting transfers between devices, named_by(): return lax.ppermute(cols, (ROW, COL), pairs)  9.8 us
    ppermute x8, waiting for transfers between devices, step(): return lax.ppermute(value, COL, pairs)  9.2 us
    ppermute x8, starting transfers between devices, step(): return lax.ppermute(value, COL, pairs)  6.73 us
    ppermute x2, waiting for transfers between devices, on_device(): lax.ppermute(left, ROW, [(r, r ^ bit) for r in range(panels)])  3.2 us
    ppermute x2, starting transfers between devices, on_device(): lax.ppermute(left, ROW, [(r, r ^ bit) for r in range(panels)])  3.08 us
  transfers between devices with their start and end apart: 12, of which 8 were waited for; matrix products, arithmetic and copies ran while one was open for 0% of the time, Pallas kernels for 43%

profile of v3, /device:TPU:0, one launch (start us, length us, event | category | flops | bytes accessed | tf_op | source)
XLA Modules:
  0.0 67.4 jit_solution(211208637608760557)
XLA Ops:
  0.0 5.0 %collective-permute-start = (s32[1,4,16]{2,1,0:T(4,128)}, s32[1,4,16]{2,1,0:T(4,128)S(1)}, u32[]{:S(2)}, u32[]{:S(2)}) collective-permute-start(s32[1,4,16]{2,1,0:T(4,128)} %bitcast.32), channel_id=1, source_target_pairs={{0,20},{1,21},{2,22},{3,23},{4,16},{5,17},{6,18},{7,19},{8,28},{9,... | collective-permute-start | bytes 776 | tf_op jit(solution)/shard_map/ppermute | solution.py:418
  5.0 0.1 stack.23.refs_0_
  5.1 1.3 %prepare.1 = (bf16[32,1024]{1,0:T(8,128)(2,1)S(1)}, s32[1,4,16]{2,1,0:T(4,128)S(1)}) custom-call(s32[5]{0:T(128)S(1)} %stack.23.refs_0_, s32[1,4,16]{2,1,0:T(4,128)} %bitcast.33, f32[4,1024]{1,0:T(4,128)} %bitcast.30, s32[4,1024]{1,0:T(4,128)} %bitcast.31), custom_call_target="tpu_custom_call" | custom-call | flops 20000000000 | bytes 1024 | tf_op jit(solution)/shard_map/prepare/pallas_call | solution.py:74
  6.4 0.4 collective-permute-done.refs_1_
  6.8 4.8 %collective-permute-start.1 = (s32[2,4,16]{2,1,0:T(4,128)S(1)}, s32[2,4,16]{2,1,0:T(4,128)S(1)}, u32[]{:S(2)}, u32[]{:S(2)}) collective-permute-start(s32[2,4,16]{2,1,0:T(4,128)S(1)} %join.4.refs_1_.refs_2_), channel_id=1, source_target_pairs={{0,14},{1,15},{2,8},{3,9},{4,10},{5,11},{6,12},{7,13},{8,22},{9,23... | collective-permute-start | bytes 1544 | tf_op jit(solution)/shard_map/ppermute | solution.py:418
  11.6 0.0 copy-start
  11.6 0.0 copy-start.1
  11.6 2.6 %answer.4 = (bf16[1040,128]{1,0:T(8,128)(2,1)}, bf16[1040,128]{1,0:T(8,128)(2,1)}) custom-call(s32[5]{0:T(128)S(1)} %stack.23.refs_0_, s32[2,4,16]{2,1,0:T(4,128)S(1)} %join.4.refs_1_.refs_2_, s32[2,4,16]{2,1,0:T(4,128)S(1)} %join.4.refs_1_.refs_2_, bf16[32,1024]{1,0:T(8,128)(2,1)S(1)} %get-tuple-element.17.refs_3_.refs_5_.refs_6_, ...), custom_call_target="tpu_custom_call" | custom-call | flops 20000000000 | bytes 1024 | tf_op jit(solution)/shard_map/answer/pallas_call | solution.py:74
  14.2 0.1 collective-permute-start.6
  14.3 0.9 %collective-permute-start.7 = (bf16[1040,128]{1,0:T(8,128)(2,1)}, bf16[1040,128]{1,0:T(8,128)(2,1)}, u32[]{:S(2)}, u32[]{:S(2)}) collective-permute-start(bf16[1040,128]{1,0:T(8,128)(2,1)} %get-tuple-element.18.refs_3_.refs_5_), channel_id=1, source_target_pairs={{0,4},{1,5},{2,6},{3,7},{4,0},{5,1},{6,2},{7,3},{8,12},{9,13},{10,... | collective-permute-start | bytes 798728 | tf_op jit(solution)/shard_map/ppermute | solution.py:409
  15.2 0.0 collective-permute-done.1.refs_4_.refs_1_.refs_2_.refs_5_
  15.2 0.0 copy-done
  15.2 0.0 copy-done.1
  15.2 0.6 split.1
  15.9 1.9 %collective-permute-start.2 = (bf16[1,272,128]{2,1,0:T(8,128)(2,1)S(1)}, bf16[1,272,128]{2,1,0:T(8,128)(2,1)S(1)}, u32[]{:S(2)}, u32[]{:S(2)}) collective-permute-start(bf16[1,272,128]{2,1,0:T(8,128)(2,1)S(1)} %get-tuple-element.20), channel_id=1, source_target_pairs={{0,1},{1,0},{2,3},{3,2},{4,5},{5,4},{6,7},{7,6},{8,9},{9,8},{10,11... | collective-permute-start | bytes 208904 | tf_op jit(solution)/shard_map/ppermute | solution.py:409
  17.8 2.3 %answer.5.refs_5_ = bf16[1040,128]{1,0:T(8,128)(2,1)} custom-call(s32[5]{0:T(128)S(1)} %stack.23.refs_0_, s32[2,4,16]{2,1,0:T(4,128)S(1)} %collective-permute-done.1.refs_4_.refs_1_.refs_2_.refs_5_, s32[2,4,16]{2,1,0:T(4,128)S(1)} %collective-permute-done.1.refs_4_.refs_1_.refs_2_.refs_5_, bf16[32,1024]{1,0:T(8,128)(2,1)S(1)} %get-tuple-element.17.refs_3_.refs_5_.refs_6_, ...), custom_call_target="tpu_custom_call" | custom-call | flops 20000000000 | bytes 1024 | tf_op jit(solution)/shard_map/answer/pallas_call | solution.py:74
  20.1 0.1 collective-permute-start.8
  20.1 2.3 %answer.6.refs_6_ = bf16[1040,128]{1,0:T(8,128)(2,1)} custom-call(s32[5]{0:T(128)S(1)} %stack.23.refs_0_, s32[2,4,16]{2,1,0:T(4,128)S(1)} %collective-permute-done.1.refs_4_.refs_1_.refs_2_.refs_5_, s32[2,4,16]{2,1,0:T(4,128)S(1)} %collective-permute-done.1.refs_4_.refs_1_.refs_2_.refs_5_, bf16[32,1024]{1,0:T(8,128)(2,1)S(1)} %get-tuple-element.17.refs_3_.refs_5_.refs_6_, ...), custom_call_target="tpu_custom_call" | custom-call | flops 20000000000 | bytes 1024 | tf_op jit(solution)/shard_map/answer/pallas_call | solution.py:74
  22.4 0.7 %collective-permute-start.9 = (bf16[1040,128]{1,0:T(8,128)(2,1)}, bf16[1040,128]{1,0:T(8,128)(2,1)}, u32[]{:S(2)}, u32[]{:S(2)}) collective-permute-start(bf16[1040,128]{1,0:T(8,128)(2,1)} %answer.6.refs_6_), channel_id=1, source_target_pairs={{0,3},{1,2},{2,5},{3,4},{4,7},{5,6},{6,1},{7,0},{8,11},{9,10},{10,... | collective-permute-start | bytes 798728 | tf_op jit(solution)/shard_map/ppermute | solution.py:409
  23.1 0.0 collective-permute-done.2.refs_1_
  23.1 1.6 %collective-permute-start.3 = (bf16[2,272,128]{2,1,0:T(8,128)(2,1)S(1)}, bf16[2,272,128]{2,1,0:T(8,128)(2,1)S(1)}, u32[]{:S(2)}, u32[]{:S(2)}) collective-permute-start(bf16[2,272,128]{2,1,0:T(8,128)(2,1)S(1)} %join.5.refs_0_.refs_1_), channel_id=1, source_target_pairs={{0,8},{8,0},{16,24},{24,16},{1,9},{9,1},{17,25},{25,17},{2,10},{10... | collective-permute-start | bytes 417800 | tf_op jit(solution)/shard_map/ppermute | solution.py:447
  24.7 4.2 %own_blocks.1 = (f32[8,128,32,128]{3,2,1,0:T(8,128)S(1)}, bf16[1040,128]{1,0:T(8,128)(2,1)S(1)}) custom-call(s32[5]{0:T(128)S(1)} %stack.23.refs_0_, s32[1,4,16]{2,1,0:T(4,128)S(1)} %get-tuple-element.16.refs_0_.refs_1_.refs_2_, s32[1,4,16]{2,1,0:T(4,128)S(1)} %get-tuple-element.16.refs_0_.refs_1_.refs_2_, ...), custom_call_target="tpu_custom_call" | custom-call | flops 20000000000 | bytes 1024 | tf_op jit(solution)/shard_map/own_blocks/pallas_call | solution.py:74
  28.9 0.2 collective-permute-done.3.refs_1_
  29.1 0.0 collective-permute-start.5
  29.1 1.5 %collective-permute-done.5.refs_3_ = bf16[1040,128]{1,0:T(8,128)(2,1)S(1)} collective-permute-done((bf16[1040,128]{1,0:T(8,128)(2,1)S(1)}, bf16[1040,128]{1,0:T(8,128)(2,1)S(1)}, u32[]{:S(2)}, u32[]{:S(2)}) %collective-permute-start.5) | collective-permute-done | bytes 266272 | tf_op jit(solution)/shard_map/ppermute | solution.py:409
  30.6 1.5 %collective-permute-start.4 = (bf16[4,272,128]{2,1,0:T(8,128)(2,1)S(1)}, bf16[4,272,128]{2,1,0:T(8,128)(2,1)S(1)}, u32[]{:S(2)}, u32[]{:S(2)}) collective-permute-start(bf16[4,272,128]{2,1,0:T(8,128)(2,1)S(1)} %join.6.refs_0_), channel_id=1, source_target_pairs={{0,16},{8,24},{16,0},{24,8},{1,17},{9,25},{17,1},{25,9},{2,18},{10... | collective-permute-start | bytes 835592 | tf_op jit(solution)/shard_map/ppermute | solution.py:447
  32.2 2.6 %add_messages.6 = (f32[8,128,32,128]{3,2,1,0:T(8,128)S(1)}, bf16[1040,128]{1,0:T(8,128)(2,1)S(1)}) custom-call(s32[5]{0:T(128)S(1)} %stack.23.refs_0_, bf16[2,272,128]{2,1,0:T(8,128)(2,1)S(1)} %join.5.refs_0_.refs_1_, f32[8,128,32,128]{3,2,1,0:T(8,128)S(1)} %get-tuple-element.21.refs_2_, ...), custom_call_target="tpu_custom_call", output_to_operand_aliasing={{0}: (2, {})} | custom-call | flops 20000000000 | bytes 1024 | tf_op jit(solution)/shard_map/add_messages/pallas_call | solution.py:74
  34.7 1.6 %answer.7.refs_4_ = bf16[1040,128]{1,0:T(8,128)(2,1)S(1)} custom-call(s32[5]{0:T(128)S(1)} %stack.23.refs_0_, s32[2,4,16]{2,1,0:T(4,128)S(1)} %collective-permute-done.1.refs_4_.refs_1_.refs_2_.refs_5_, s32[2,4,16]{2,1,0:T(4,128)S(1)} %collective-permute-done.1.refs_4_.refs_1_.refs_2_.refs_5_, ...), custom_call_target="tpu_custom_call" | custom-call | flops 20000000000 | bytes 1024 | tf_op jit(solution)/shard_map/answer/pallas_call | solution.py:74
  36.3 3.0 %collective-permute-done.4.refs_1_ = bf16[4,272,128]{2,1,0:T(8,128)(2,1)S(1)} collective-permute-done((bf16[4,272,128]{2,1,0:T(8,128)(2,1)S(1)}, bf16[4,272,128]{2,1,0:T(8,128)(2,1)S(1)}, u32[]{:S(2)}, u32[]{:S(2)}) %collective-permute-start.4) | collective-permute-done | bytes 278560 | tf_op jit(solution)/shard_map/ppermute | solution.py:447
  39.3 3.1 %collective-permute-start.10 = (bf16[1040,128]{1,0:T(8,128)(2,1)S(1)}, bf16[1040,128]{1,0:T(8,128)(2,1)S(1)}, u32[]{:S(2)}, u32[]{:S(2)}) collective-permute-start(bf16[1040,128]{1,0:T(8,128)(2,1)S(1)} %get-tuple-element.25.refs_5_), channel_id=1, source_target_pairs={{0,6},{1,7},{2,0},{3,1},{4,2},{5,3},{6,4},{7,5},{8,14},{9,15},{10,... | collective-permute-start | bytes 798728 | tf_op jit(solution)/shard_map/ppermute | solution.py:409
  42.5 2.6 %collective-permute-done.6.refs_3_ = bf16[1040,128]{1,0:T(8,128)(2,1)} collective-permute-done((bf16[1040,128]{1,0:T(8,128)(2,1)}, bf16[1040,128]{1,0:T(8,128)(2,1)}, u32[]{:S(2)}, u32[]{:S(2)}) %collective-permute-start.6) | collective-permute-done | bytes 266272 | tf_op jit(solution)/shard_map/ppermute | solution.py:409
  45.1 0.0 collective-permute-start.11
  45.1 2.6 %add_messages.7.refs_2_ = f32[8,128,32,128]{3,2,1,0:T(8,128)S(1)} custom-call(s32[5]{0:T(128)S(1)} %stack.23.refs_0_, bf16[8,272,128]{2,1,0:T(8,128)(2,1)S(1)} %join.7.refs_1_, f32[8,128,32,128]{3,2,1,0:T(8,128)S(1)} %get-tuple-element.23.refs_2_, bf16[1040,128]{1,0:T(8,128)(2,1)} %collective-permute-done.6.refs_3_, ...), custom_call_target="tpu_custom_call", output_to_operand_aliasing={{}: (2, {})} | custom-call | flops 20000000000 | bytes 1024 | tf_op jit(solution)/shard_map/add_messages/pallas_call | solution.py:74
  47.7 2.9 %collective-permute-done.7.refs_3_ = bf16[1040,128]{1,0:T(8,128)(2,1)} collective-permute-done((bf16[1040,128]{1,0:T(8,128)(2,1)}, bf16[1040,128]{1,0:T(8,128)(2,1)}, u32[]{:S(2)}, u32[]{:S(2)}) %collective-permute-start.7) | collective-permute-done | bytes 266272 | tf_op jit(solution)/shard_map/ppermute | solution.py:409
  50.6 2.6 %add_messages.8.refs_2_ = f32[8,128,32,128]{3,2,1,0:T(8,128)S(1)} custom-call(s32[5]{0:T(128)S(1)} %stack.23.refs_0_, bf16[8,272,128]{2,1,0:T(8,128)(2,1)S(1)} %join.7.refs_1_, f32[8,128,32,128]{3,2,1,0:T(8,128)S(1)} %add_messages.7.refs_2_, bf16[1040,128]{1,0:T(8,128)(2,1)} %collective-permute-done.7.refs_3_), custom_call_target="tpu_custom_call", output_to_operand_aliasing={{}: (2, {})} | custom-call | flops 20000000000 | bytes 1024 | tf_op jit(solution)/shard_map/add_messages/pallas_call | solution.py:74
  53.2 0.0 collective-permute-done.8.refs_3_
  53.2 2.6 %add_messages.9.refs_2_ = f32[8,128,32,128]{3,2,1,0:T(8,128)S(1)} custom-call(s32[5]{0:T(128)S(1)} %stack.23.refs_0_, bf16[8,272,128]{2,1,0:T(8,128)(2,1)S(1)} %join.7.refs_1_, f32[8,128,32,128]{3,2,1,0:T(8,128)S(1)} %add_messages.8.refs_2_, bf16[1040,128]{1,0:T(8,128)(2,1)} %collective-permute-done.8.refs_3_), custom_call_target="tpu_custom_call", output_to_operand_aliasing={{}: (2, {})} | custom-call | flops 20000000000 | bytes 1024 | tf_op jit(solution)/shard_map/add_messages/pallas_call | solution.py:74
  55.9 0.0 collective-permute-done.9.refs_3_
  55.9 0.4 collective-permute-done.10.refs_4_
  56.3 3.7 %add_messages.10.refs_2_ = f32[8,128,32,128]{3,2,1,0:T(8,128)S(1)} custom-call(s32[5]{0:T(128)S(1)} %stack.23.refs_0_, bf16[8,272,128]{2,1,0:T(8,128)(2,1)S(1)} %join.7.refs_1_, f32[8,128,32,128]{3,2,1,0:T(8,128)S(1)} %add_messages.9.refs_2_, bf16[1040,128]{1,0:T(8,128)(2,1)} %collective-permute-done.9.refs_3_, ...), custom_call_target="tpu_custom_call", output_to_operand_aliasing={{}: (2, {})} | custom-call | flops 20000000000 | bytes 1024 | tf_op jit(solution)/shard_map/add_messages/pallas_call | solution.py:74
  60.0 1.8 %collective-permute-done.11.refs_3_ = bf16[1040,128]{1,0:T(8,128)(2,1)S(1)} collective-permute-done((bf16[1040,128]{1,0:T(8,128)(2,1)S(1)}, bf16[1040,128]{1,0:T(8,128)(2,1)S(1)}, u32[]{:S(2)}, u32[]{:S(2)}) %collective-permute-start.11) | collective-permute-done | bytes 266272 | tf_op jit(solution)/shard_map/ppermute | solution.py:409
  61.8 5.5 %add_messages.11 = (f32[8,128,32,128]{3,2,1,0:T(8,128)S(1)}, bf16[8,32,16384]{2,1,0:T(8,128)(2,1)}) custom-call(s32[5]{0:T(128)S(1)} %stack.23.refs_0_, bf16[8,272,128]{2,1,0:T(8,128)(2,1)S(1)} %join.7.refs_1_, f32[8,128,32,128]{3,2,1,0:T(8,128)S(1)} %add_messages.10.refs_2_, ...), custom_call_target="tpu_custom_call", output_to_operand_aliasing={{0}: (2, {})} | custom-call | flops 20000000000 | bytes 1024 | tf_op jit(solution)/shard_map/add_messages/pallas_call | solution.py:74
  (4 shorter events, 0.1 us)
Async XLA Ops:
  0.0 6.8 %collective-permute-start = (s32[1,4,16]{2,1,0:T(4,128)}, s32[1,4,16]{2,1,0:T(4,128)S(1)}, u32[]{:S(2)}, u32[]{:S(2)}) collective-permute-start(s32[1,4,16]{2,1,0:T(4,128)} %bitcast.32), channel_id=1, source_target_pairs={{0,20},{1,21},{2,22},{3,23},{4,16},{5,17},{6,18},{7,19},{8,28},{9,... | collective-permute-start | bytes 776 | tf_op jit(solution)/shard_map/ppermute | solution.py:418
  6.8 8.5 %collective-permute-start.1 = (s32[2,4,16]{2,1,0:T(4,128)S(1)}, s32[2,4,16]{2,1,0:T(4,128)S(1)}, u32[]{:S(2)}, u32[]{:S(2)}) collective-permute-start(s32[2,4,16]{2,1,0:T(4,128)S(1)} %join.4.refs_1_.refs_2_), channel_id=1, source_target_pairs={{0,14},{1,15},{2,8},{3,9},{4,10},{5,11},{6,12},{7,13},{8,22},{9,23... | collective-permute-start | bytes 1544 | tf_op jit(solution)/shard_map/ppermute | solution.py:418
  11.6 3.7 %copy-start = (bf16[1,1,16,32,128]{4,3,2,1,0:T(8,128)(2,1)S(1)}, bf16[1,1,16,32,128]{4,3,2,1,0:T(8,128)(2,1)}, u32[]{:S(2)}) copy-start(bf16[1,1,16,32,128]{4,3,2,1,0:T(8,128)(2,1)} %param.6) | copy-start | bytes 393220
  11.6 3.7 %copy-start.1 = (f32[1,1,16,4]{2,3,1,0:T(4,128)S(1)}, f32[1,1,16,4]{2,3,1,0:T(4,128)}, u32[]{:S(2)}) copy-start(f32[1,1,16,4]{2,3,1,0:T(4,128)} %param.7) | copy-start | bytes 772
  14.2 30.8 %collective-permute-start.6 = (bf16[1040,128]{1,0:T(8,128)(2,1)}, bf16[1040,128]{1,0:T(8,128)(2,1)}, u32[]{:S(2)}, u32[]{:S(2)}) collective-permute-start(bf16[1040,128]{1,0:T(8,128)(2,1)} %get-tuple-element.24), channel_id=1, source_target_pairs={{0,5},{1,4},{2,7},{3,6},{4,1},{5,0},{6,3},{7,2},{8,13},{9,12},{10,... | collective-permute-start | bytes 798728 | tf_op jit(solution)/shard_map/ppermute | solution.py:409
  14.3 36.3 %collective-permute-start.7 = (bf16[1040,128]{1,0:T(8,128)(2,1)}, bf16[1040,128]{1,0:T(8,128)(2,1)}, u32[]{:S(2)}, u32[]{:S(2)}) collective-permute-start(bf16[1040,128]{1,0:T(8,128)(2,1)} %get-tuple-element.18.refs_3_.refs_5_), channel_id=1, source_target_pairs={{0,4},{1,5},{2,6},{3,7},{4,0},{5,1},{6,2},{7,3},{8,12},{9,13},{10,... | collective-permute-start | bytes 798728 | tf_op jit(solution)/shard_map/ppermute | solution.py:409
  15.9 7.2 %collective-permute-start.2 = (bf16[1,272,128]{2,1,0:T(8,128)(2,1)S(1)}, bf16[1,272,128]{2,1,0:T(8,128)(2,1)S(1)}, u32[]{:S(2)}, u32[]{:S(2)}) collective-permute-start(bf16[1,272,128]{2,1,0:T(8,128)(2,1)S(1)} %get-tuple-element.20), channel_id=1, source_target_pairs={{0,1},{1,0},{2,3},{3,2},{4,5},{5,4},{6,7},{7,6},{8,9},{9,8},{10,11... | collective-permute-start | bytes 208904 | tf_op jit(solution)/shard_map/ppermute | solution.py:409
  20.1 33.2 %collective-permute-start.8 = (bf16[1040,128]{1,0:T(8,128)(2,1)}, bf16[1040,128]{1,0:T(8,128)(2,1)}, u32[]{:S(2)}, u32[]{:S(2)}) collective-permute-start(bf16[1040,128]{1,0:T(8,128)(2,1)} %answer.5.refs_5_), channel_id=1, source_target_pairs={{0,2},{1,3},{2,4},{3,5},{4,6},{5,7},{6,0},{7,1},{8,10},{9,11},{10,... | collective-permute-start | bytes 798728 | tf_op jit(solution)/shard_map/ppermute | solution.py:409
  22.4 33.5 %collective-permute-start.9 = (bf16[1040,128]{1,0:T(8,128)(2,1)}, bf16[1040,128]{1,0:T(8,128)(2,1)}, u32[]{:S(2)}, u32[]{:S(2)}) collective-permute-start(bf16[1040,128]{1,0:T(8,128)(2,1)} %answer.6.refs_6_), channel_id=1, source_target_pairs={{0,3},{1,2},{2,5},{3,4},{4,7},{5,6},{6,1},{7,0},{8,11},{9,10},{10,... | collective-permute-start | bytes 798728 | tf_op jit(solution)/shard_map/ppermute | solution.py:409
  23.1 6.0 %collective-permute-start.3 = (bf16[2,272,128]{2,1,0:T(8,128)(2,1)S(1)}, bf16[2,272,128]{2,1,0:T(8,128)(2,1)S(1)}, u32[]{:S(2)}, u32[]{:S(2)}) collective-permute-start(bf16[2,272,128]{2,1,0:T(8,128)(2,1)S(1)} %join.5.refs_0_.refs_1_), channel_id=1, source_target_pairs={{0,8},{8,0},{16,24},{24,16},{1,9},{9,1},{17,25},{25,17},{2,10},{10... | collective-permute-start | bytes 417800 | tf_op jit(solution)/shard_map/ppermute | solution.py:447
  29.1 1.5 %collective-permute-start.5 = (bf16[1040,128]{1,0:T(8,128)(2,1)S(1)}, bf16[1040,128]{1,0:T(8,128)(2,1)S(1)}, u32[]{:S(2)}, u32[]{:S(2)}) collective-permute-start(bf16[1040,128]{1,0:T(8,128)(2,1)S(1)} %get-tuple-element.22), channel_id=1, source_target_pairs={{0,1},{1,0},{2,3},{3,2},{4,5},{5,4},{6,7},{7,6},{8,9},{9,8},{10,11... | collective-permute-start | bytes 798728 | tf_op jit(solution)/shard_map/ppermute | solution.py:409
  30.6 8.7 %collective-permute-start.4 = (bf16[4,272,128]{2,1,0:T(8,128)(2,1)S(1)}, bf16[4,272,128]{2,1,0:T(8,128)(2,1)S(1)}, u32[]{:S(2)}, u32[]{:S(2)}) collective-permute-start(bf16[4,272,128]{2,1,0:T(8,128)(2,1)S(1)} %join.6.refs_0_), channel_id=1, source_target_pairs={{0,16},{8,24},{16,0},{24,8},{1,17},{9,25},{17,1},{25,9},{2,18},{10... | collective-permute-start | bytes 835592 | tf_op jit(solution)/shard_map/ppermute | solution.py:447
  39.3 16.9 %collective-permute-start.10 = (bf16[1040,128]{1,0:T(8,128)(2,1)S(1)}, bf16[1040,128]{1,0:T(8,128)(2,1)S(1)}, u32[]{:S(2)}, u32[]{:S(2)}) collective-permute-start(bf16[1040,128]{1,0:T(8,128)(2,1)S(1)} %get-tuple-element.25.refs_5_), channel_id=1, source_target_pairs={{0,6},{1,7},{2,0},{3,1},{4,2},{5,3},{6,4},{7,5},{8,14},{9,15},{10,... | collective-permute-start | bytes 798728 | tf_op jit(solution)/shard_map/ppermute | solution.py:409
  45.1 16.7 %collective-permute-start.11 = (bf16[1040,128]{1,0:T(8,128)(2,1)S(1)}, bf16[1040,128]{1,0:T(8,128)(2,1)S(1)}, u32[]{:S(2)}, u32[]{:S(2)}) collective-permute-start(bf16[1040,128]{1,0:T(8,128)(2,1)S(1)} %answer.7.refs_4_), channel_id=1, source_target_pairs={{0,7},{1,6},{2,1},{3,0},{4,3},{5,2},{6,5},{7,4},{8,15},{9,14},{10,... | collective-permute-start | bytes 798728 | tf_op jit(solution)/shard_map/ppermute | solution.py:409
